TPU v7x, 128 devices: a whole 4x4x4 slice. The times are simulated.
128 devices in a mesh: dp: 32 (over x, y, core), seq: 4 (over z).
Axes of the slice: x: 4, y: 4, z: 4, core: 2. Of those that a mesh axis runs over, the one named last changes fastest.
Arguments:
- hidden_in: bfloat16 [2, 32, 1024, 1024], P(None, 'dp', 'seq'), may hold values from -6 to 6
- segments: int32 [2, 32, 1024], P(None, 'dp'), may hold values from 0 to 1023, as said below
- valid_mask: int32 [2, 32, 1024], P(None, 'dp'), may hold values from 0 to 1, as said below
- w_qkv: bfloat16 [1024, 3072], P(('dp', 'seq')), may hold values from -0.1875 to 0.1875
- w_out: bfloat16 [1024, 1024], P(('dp', 'seq')), may hold values from -1.5 to 1.5
- w_up: bfloat16 [1024, 4096], P(('dp', 'seq')), may hold values from -0.1875 to 0.1875
- w_down: bfloat16 [4096, 1024], P(('dp', 'seq')), may hold values from -0.09375 to 0.09375
- b_qkv: bfloat16 [3072], P(('dp', 'seq')), may hold values from -3 to 3
- b_out: bfloat16 [1024], P(('dp', 'seq')), may hold values from -3 to 3
- b_up: bfloat16 [4096], P(('dp', 'seq')), may hold values from -3 to 3
- b_down: bfloat16 [1024], P(('dp', 'seq')), may hold values from -3 to 3
- ln_gain: bfloat16 [1024], P(('dp', 'seq')), may hold values from 0.099609375 to 1.8984375
- ln_shift: bfloat16 [1024], P(('dp', 'seq')), may hold values from -3 to 3
- cotangent: bfloat16 [2, 32, 1024, 1024], P(None, 'dp', 'seq'), may hold values from -6 to 6
Outputs:
- out_hidden: bfloat16 [2, 32, 1024, 1024], P(None, 'dp', 'seq')
- grad_input: float32 [2, 32, 1024, 1024], P(None, 'dp', 'seq')
- grad_qkv: float32 [1024, 3072], P(('dp', 'seq'))
- grad_out: float32 [1024, 1024], P(('dp', 'seq'))
- grad_up: float32 [1024, 4096], P(('dp', 'seq'))
- grad_down: float32 [4096, 1024], P(('dp', 'seq'))
- grad_bqkv: float32 [3072], P(('dp', 'seq'))
- grad_bout: float32 [1024], P(('dp', 'seq'))
- grad_bup: float32 [4096], P(('dp', 'seq'))
- grad_bdown: float32 [1024], P(('dp', 'seq'))
- grad_gain: float32 [1024], P(('dp', 'seq'))
- grad_shift: float32 [1024], P(('dp', 'seq'))
Inputs may be any that keep to these rules, and one draw needn't show every extreme that they name: `segments`: along a row, segment ids start at 0 and never fall; tokens of one document are contiguous; the padding tokens form the last segment, with id 1024 - 1. `valid_mask`: along a row the ones come first and at least one zero ends it.
All inputs are finite; a program needn't handle non-finite values.
Results may differ from a plain program's by a relative error of at most 0.011.
Values may be sent and summed in bfloat16 or wider, within the bound.
No kernel may reach another device: no remote copies, remote signals or barrier semaphores. Data moves between devices by JAX's collectives and lax.ppermute only.
A program may use at most 256 MiB of HBM per device.

v0:
```python
import functools

import jax
import jax.numpy as jnp
from jax import lax
from jax.experimental import pallas as pl
from jax.experimental.pallas import tpu as pltpu
from jax.sharding import PartitionSpec as P

BF = jnp.bfloat16
F32 = jnp.float32
MB = 1 << 20
HEAD_DIM = 64
ROT = 32
NZ = 4


def dot(left, right):
    return jnp.dot(left, right, preferred_element_type=F32)


def dot_nt(left, right):
    return lax.dot_general(left, right, (((1,), (1,)), ((), ())), preferred_element_type=F32)


def dot_tn(left, right):
    return lax.dot_general(left, right, (((0,), (0,)), ((), ())), preferred_element_type=F32)


def turn(value, cos, sin, sign):
    right, left = pltpu.roll(value, 16, 1), pltpu.roll(value, 112, 1)
    first = lax.broadcasted_iota(jnp.int32, value.shape, 1) % 32 < 16
    return value * cos + jnp.where(first, left, right) * (sign * sin)


def spread(value, period):
    while period < 128:
        value = value + pltpu.roll(value, period, 1)
        period *= 2
    return value


def lay_out(value, period):
    fold = 128 // period
    lane = lax.broadcasted_iota(jnp.int32, value.shape, 1) // period
    row = lax.broadcasted_iota(jnp.int32, value.shape, 0) % fold
    value = jnp.where(lane == row, spread(value, period), 0.0)
    value = jnp.sum(value.reshape(8, fold, 128), axis=1)
    return jnp.concatenate([value[t : t + 1] for t in range(8)], axis=1)


def unpack_parameters(z, w_ref, wo_ref, vec_ref, block_s):
    rows = w_ref[:, 2816:3072].astype(F32).reshape(32, 4, 8, 256)
    for b in range(4):
        wo_ref[:, b * 256 : b * 256 + 256] = rows[:, b].reshape(256, 256).astype(BF)
    block_s[...] = w_ref[:, 3072:3200].astype(F32)

    def kind(k, first=0, count=128):
        return block_s[pl.ds(first * 8 + k, count, stride=8), :]

    vec_ref[0:1, :] = lay_out(kind(4), 8)
    vec_ref[1:2, :] = lay_out(kind(5), 8)
    vec_ref[2:3, :] = lay_out(kind(2, z * 32, 32), 32)
    vec_ref[4:5, :] = lay_out(kind(1) + kind(3), 8)
    lane = lax.broadcasted_iota(jnp.int32, (128, 128), 1)
    row = lax.broadcasted_iota(jnp.int32, (128, 128), 0)
    qkv = kind(0)
    groups = []
    for g in range(3):
        here = jnp.where(lane < 8, pltpu.roll(qkv, 128 - 8 * g, 1) if g else qkv, 0.0)
        groups.append(spread(here, 8))
    for part in range(3):
        for half in range(2):
            want = (part * 8 + z * 2 + half) * 16 + lane // 8
            total = jnp.zeros((128, 128), F32)
            for g in range(3):
                total = total + jnp.where(3 * row + g == want, groups[g], 0.0)
            at = part * 256 + half * 128
            vec_ref[3:4, at : at + 128] = jnp.sum(total, axis=0, keepdims=True)


def front_kernel(known, z_ref, *rest):
    z = z_ref[0]
    step = pl.program_id(0)
    if not known:
        rest, (wo_ref, vec_ref, block_s) = rest[:-3], rest[-3:]
    x_ref, c_ref, n_ref, act_ref, dup_ref, q_ref, k_ref, v_ref, dm_ref, stat_ref, sum_ref = rest[
        -11:
    ]
    tile = x_ref.shape[1]
    for at, piece in enumerate(rest[:NZ]):

        @pl.when(step == at)
        def _(piece=piece):
            x_ref[0], c_ref[0] = piece[:tile], piece[tile:]

    w_ref = rest[NZ]
    if known:
        wo_ref, vec_ref, cos_ref, sin_ref = rest[NZ + 1 : NZ + 5]
    else:
        cos_ref, sin_ref = rest[NZ + 1 : NZ + 3]

        @pl.when(step == 0)
        def _():
            unpack_parameters(z, w_ref, wo_ref, vec_ref, block_s)

    gain_ref, shift_ref, bu_ref, bq_ref = [vec_ref.at[k : k + 1] for k in range(4)]

    @pl.when(step == 0)
    def _():
        sum_ref[...] = jnp.zeros_like(sum_ref)

    def put(ref, value):
        for r in range(tile // 256):
            row = lax.rem(pl.program_id(0) * (tile // 256) + r + z, 4) * 256
            ref[0, pl.ds(pl.multiple_of(row, 256), 256), :] = value[r * 256 : r * 256 + 256]

    def d_act_of(j):
        return dot_nt(c_ref[0], w_ref[j * 256 : j * 256 + 256, 1792:2816])

    def in_of(j):
        return dot(n_ref[0], w_ref[:, j * 256 : j * 256 + 256])

    d_act = d_act_of(0)
    d_mixed = dot_nt(c_ref[0], wo_ref[...])
    x = x_ref[0].astype(F32)
    average = jnp.mean(x, axis=-1, keepdims=True)
    centered = x - average
    spread = jnp.mean(centered * centered, axis=-1, keepdims=True)
    rs = lax.rsqrt(spread + 1e-05)
    stat_ref[0, :, 0:1] = average
    stat_ref[0, :, 1:2] = rs
    n_ref[0] = (centered * rs * gain_ref[...] + shift_ref[...]).astype(BF)
    put(dm_ref, d_mixed.astype(BF))
    up = in_of(0)
    k0 = 0.7978845608028654
    k1 = k0 * 0.044715
    for j in range(4):
        cols = slice(j * 256, j * 256 + 256)
        if j < 3:
            next_up, next_act = in_of(j + 1), d_act_of(j + 1)
        else:
            q, k, v = in_of(4), in_of(5), in_of(6)
        up = up + bu_ref[:, cols]
        square = up * up
        half = 0.5 + 0.5 * jnp.tanh(up * (k0 + k1 * square))
        act = up * half
        slope = half + 2.0 * act * (1.0 - half) * (k0 + 3.0 * k1 * square)
        d_up = (slope * d_act).astype(BF)
        act_ref[0, :, cols] = act.astype(BF)
        dup_ref[0, :, cols] = d_up
        back = d_up.astype(F32)
        sum_ref[:, cols] += jnp.sum(back.reshape(back.shape[0] // 8, 8, 256), axis=0)
        up, d_act = next_up, next_act
    tabs = (cos_ref[0], sin_ref[0])
    def turn_both(value):
        return jnp.concatenate(
            [turn(value[:, h : h + 128], *tabs, 1.0) for h in (0, 128)], axis=1
        ).astype(BF)

    q = turn_both(q + bq_ref[:, 0:256]) * BF(0.125)
    put(q_ref, q)
    put(k_ref, turn_both(k + bq_ref[:, 256:512]))
    put(v_ref, (v + bq_ref[:, 512:768]).astype(BF))


ANY = pl.BlockSpec(memory_space=pl.ANY)
QUICK = pl.CostEstimate(flops=1024, bytes_accessed=1024, transcendentals=0)


def front(z, pieces, weights, known, cos, sin, after, limit):
    tile, d = pieces[0].shape[-2] // 2, pieces[0].shape[-1]
    n = tile * NZ

    def tok(width):
        return pl.BlockSpec((1, tile, width), lambda j, z: (0, j, 0))

    def turned(width):
        return pl.BlockSpec((1, tile, width), lambda j, z: (0, lax.rem(j + z[0], NZ), 0))

    def row(width):
        return pl.BlockSpec((1, n, width), lambda j, z: (0, 0, 0))

    def whole(a):
        return pl.BlockSpec(a.shape, lambda j, z: (0, 0), pipeline_mode=pl.Buffered(1))

    def keep(*shape):
        return pl.BlockSpec(shape, lambda j, z: (0, 0))

    first = [whole(a) for a in pieces]
    fixed = (weights, *known)
    out_specs = [tok(d)] * 5 + [row(256)] * 4 + [tok(128), keep(8, 1024)]
    out_shape = [jax.ShapeDtypeStruct((1, n, w), BF) for w in [d] * 5 + [256] * 4]
    out_shape += [jax.ShapeDtypeStruct((1, n, 128), F32), jax.ShapeDtypeStruct((8, 1024), F32)]
    scratch = []
    if not known:
        out_specs += [keep(256, d), keep(8, d)]
        out_shape += [jax.ShapeDtypeStruct((256, d), BF), jax.ShapeDtypeStruct((8, d), F32)]
        scratch = [pltpu.VMEM((1024, 128), F32)]
    return pl.pallas_call(
        functools.partial(front_kernel, bool(known)),
        grid_spec=pltpu.PrefetchScalarGridSpec(
            num_scalar_prefetch=1,
            grid=(NZ,),
            in_specs=first + [whole(a) for a in fixed] + [turned(128)] * 2 + [ANY] * len(after),
            out_specs=out_specs,
            scratch_shapes=scratch,
        ),
        out_shape=out_shape,
        compiler_params=pltpu.CompilerParams(vmem_limit_bytes=limit * MB),
        cost_estimate=QUICK,
        name="front",
    )(z, *pieces, *fixed, cos, sin, *after)


def attend_kernel(
    z_ref, q_ref, k_ref, v_ref, dm_ref, row_ref, key_ref, cos_ref, sin_ref, *rest,
):
    mixed_ref, dqkv_ref, sum_ref, bias_s, s_s, dp_s, p_s, ds_s, qm_s, dmm_s, dk_s, dv_s = rest[-12:]
    B = 256
    z = z_ref[0]
    sum_ref[...] = jnp.zeros_like(sum_ref)

    def put(part, a, value):
        rows = pl.ds(pl.multiple_of(lax.rem(a - z + 4, 4) * B, B), B)
        if part is None:
            mixed_ref[0, rows, :] = value
        else:
            dqkv_ref[0, part, rows, :] = value
            sum_ref[part, 0:1, :] += jnp.sum(value.astype(F32), axis=0, keepdims=True)

    key_col = key_ref[0].T
    lane_head = lax.broadcasted_iota(jnp.int32, (B, 128), 1) // 64
    diff = lax.broadcasted_iota(jnp.int32, (B, B), 0) - lax.broadcasted_iota(jnp.int32, (B, B), 1)

    def prepare(aq):
        par, n, here = aq % 2, (aq + 1) * B, slice(aq * B, aq * B + B)
        bias = jnp.where(key_col[0:n, 0:1] == row_ref[0, 0:1, here], 0.0, -1e30)
        if aq:
            bias_s[par, 0 : aq * B, :] = bias[: aq * B]
        edge = jnp.where(diff <= 0, bias[aq * B :], -1e30)
        bias_s[par, here, :] = jnp.where(diff == 0, 0.0, edge)
        q_all, d_all = q_ref[0, here, :], dm_ref[0, here, :]
        for h in range(2):
            cols = slice(h * B, h * B + B)
            qm_s[par, cols, :] = jnp.where(lane_head == h, q_all, jnp.zeros_like(q_all))
            dmm_s[par, cols, :] = jnp.where(lane_head == h, d_all, jnp.zeros_like(d_all))

    def products(aq, h):
        par, n, cols = aq % 2, (aq + 1) * B, slice(h * B, h * B + B)
        s = dot_nt(k_ref[0, 0:n, :], qm_s[par, cols, :]) + bias_s[par, 0:n, :]
        s_s[h, 0:n] = s
        dp_s[h, 0:n] = dot_nt(v_ref[0, 0:n, :], dmm_s[par, cols, :])
        return jnp.max(s, axis=0, keepdims=True)

    def soften(aq, h, top):
        par, n, cols = aq % 2, (aq + 1) * B, slice(h * B, h * B + B)
        e = jnp.exp(s_s[h, 0:n] - top)
        s_s[h, 0:n] = e
        inv = 1.0 / jnp.sum(e, axis=0, keepdims=True)
        mean = jnp.sum(e * dp_s[h, 0:n], axis=0, keepdims=True) * inv
        p = s_s[h, 0:n] * inv
        p_s[par, 0:n, cols] = p.astype(BF)
        ds_s[par, 0:n, cols] = (p * (dp_s[h, 0:n] - mean)).astype(BF)

    def pick(value):
        return jnp.where(lane_head == 0, value[0:B], value[B:])

    def gather(aq, part):
        par, n, here = aq % 2, (aq + 1) * B, slice(aq * B, aq * B + B)
        if part == 0:
            put(None, aq, pick(dot_tn(p_s[par, 0:n, :], v_ref[0, 0:n, :])).astype(BF))
        elif part == 1:
            dq = pick(dot_tn(ds_s[par, 0:n, :], k_ref[0, 0:n, :])) * 0.125
            put(0, aq, turn(dq, cos_ref[0, here, :], sin_ref[0, here, :], -1.0).astype(BF))
        else:
            left, right, to = (p_s, dmm_s, dv_s) if part == 2 else (ds_s, qm_s, dk_s)
            value = dot(left[par, 0:n, :], right[par])
            if aq:
                to[0 : aq * B, :] += value[: aq * B]
            to[here, :] = value[aq * B :]

    prepare(0)
    top = products(0, 0)
    for aq in range(4):
        ahead = products(aq, 1)
        if aq:
            gather(aq - 1, 0)
            gather(aq - 1, 1)
        soften(aq, 0, top)
        if aq:
            gather(aq - 1, 2)
            gather(aq - 1, 3)
        if aq < 3:
            prepare(aq + 1)
            top = products(aq + 1, 0)
        soften(aq, 1, ahead)
    for part in range(4):
        gather(3, part)
    for a in range(4):
        here = slice(a * B, a * B + B)
        put(1, a, turn(dk_s[here, :], cos_ref[0, here, :], sin_ref[0, here, :], -1.0).astype(BF))
        put(2, a, dv_s[here, :].astype(BF))


def attend(z, q, k, v, dm, seg_row, seg_key, cos, sin, after, limit):
    n = q.shape[1]
    half = pl.BlockSpec((1, n, 128), lambda g, z: (0, 0, g))
    table = pl.BlockSpec((1, n, 128), lambda g, z: (0, 0, 0))
    line = pl.BlockSpec((1, 8, n), lambda g, z: (0, 0, 0))
    S = pltpu.VMEM
    return pl.pallas_call(
        attend_kernel,
        grid_spec=pltpu.PrefetchScalarGridSpec(
            num_scalar_prefetch=1,
            grid=(2,),
            in_specs=[half] * 4 + [line] * 2 + [table] * 2 + [ANY] * len(after),
            out_specs=[
                half,
                pl.BlockSpec((1, 3, n, 128), lambda g, z: (0, 0, 0, g)),
                pl.BlockSpec((3, 8, 128), lambda g, z: (0, 0, g)),
            ],
            scratch_shapes=[
                S((2, n, 256), F32), S((2, n, 256), F32), S((2, n, 256), F32),
                S((2, n, 512), BF), S((2, n, 512), BF),
                S((2, 512, 128), BF), S((2, 512, 128), BF),
                S((n, 128), F32), S((n, 128), F32),
            ],
        ),
        out_shape=[
            jax.ShapeDtypeStruct((1, n, 256), BF),
            jax.ShapeDtypeStruct((1, 3, n, 256), BF),
            jax.ShapeDtypeStruct((3, 8, 256), F32),
        ],
        compiler_params=pltpu.CompilerParams(vmem_limit_bytes=limit * MB),
        cost_estimate=QUICK,
        name="attend",
    )(z, q, k, v, dm, seg_row, seg_key, cos, sin, *after)


def back_kernel(
    z_ref, act_ref, mix_ref, dup_ref, dqkv_ref, x_ref, stat_ref, wd_ref, wo_ref, wi_ref, *rest,
):
    cut, gain_ref, shift_ref = rest[-3:]
    z = z_ref[0]
    out = dot(act_ref[0], wd_ref[...]) + dot(mix_ref[0], wo_ref[...])
    dn = dot_nt(dup_ref[0], wi_ref[:, 0:1024])
    for part in range(3):
        at = 1024 + part * 256
        dn = dn + dot_nt(dqkv_ref[0, part], wi_ref[:, at : at + 256])
    xhat = (x_ref[0].astype(F32) - stat_ref[0, :, 0:1]) * stat_ref[0, :, 1:2]
    gain_ref[...] = jnp.sum((dn * xhat).reshape(-1, 8, 256), axis=0)
    shift_ref[...] = jnp.sum(dn.reshape(-1, 8, 256), axis=0)
    for r in range(NZ):
        rows = slice(r * 256, r * 256 + 256)
        first = pl.multiple_of(lax.rem(r + z, NZ) * 512, 512)
        cut[pl.ds(first, 256), :] = out[rows].astype(BF)
        cut[pl.ds(first + 256, 256), :] = dn[rows].astype(BF)


def back(z, act, mixed, d_up, d_qkv, x, stat, weights, w_o, after, limit):
    def rows(a):
        return pl.BlockSpec(a.shape, lambda j, z: (0,) * a.ndim, pipeline_mode=pl.Buffered(1))

    def cols(n, first=0):
        return pl.BlockSpec((n, 256), lambda j, z: (0, first + j))

    return pl.pallas_call(
        back_kernel,
        grid_spec=pltpu.PrefetchScalarGridSpec(
            num_scalar_prefetch=1,
            grid=(4,),
            in_specs=[rows(a) for a in (act, mixed, d_up, d_qkv)]
            + [
                pl.BlockSpec((1, 1024, 256), lambda j, z: (0, 0, j)),
                rows(stat),
                cols(1024, 7),
                cols(256),
                pl.BlockSpec((256, 1792), lambda j, z: (j, 0)),
            ]
            + [ANY] * len(after),
            out_specs=[cols(2048)] + [cols(8)] * 2,
        ),
        out_shape=[jax.ShapeDtypeStruct((2048, 1024), BF)]
        + [jax.ShapeDtypeStruct((8, 1024), F32)] * 2,
        compiler_params=pltpu.CompilerParams(vmem_limit_bytes=limit * MB),
        cost_estimate=QUICK,
        name="back",
    )(z, act, mixed, d_up, d_qkv, x, stat, weights, w_o, weights, *after)


def put_halves(c, value, own_ref, other_ref, lo):
    value = value.reshape(4, 2, 32, value.shape[1])
    first, second = [value[:, k].reshape(128, value.shape[3]) for k in range(2)]
    hi = lo + value.shape[3]
    own_ref[:, lo:hi] = jnp.where(c == 0, first, second).astype(BF)
    other_ref[:, lo:hi] = jnp.where(c == 0, second, first).astype(BF)


def grads_mlp0_kernel(n_ref, dup_ref, act_ref, cot_ref, *rest):
    rest[-1][:, 0:1024] = dot_tn(n_ref[0], dup_ref[0]).astype(BF)
    rest[-1][:, 1024:2048] = dot_tn(act_ref[0], cot_ref[0]).astype(BF)


def grads_mlp1_kernel(c_ref, n_ref, dup_ref, act_ref, cot_ref, sum_ref, own_ref, other_ref):
    c = c_ref[0]
    up = sum_ref[:, 0:1024].astype(F32) + dot_tn(n_ref[0], dup_ref[0])
    put_halves(c, up, own_ref, other_ref, 0)
    down = sum_ref[:, 1024:2048].astype(F32) + dot_tn(act_ref[0], cot_ref[0])
    put_halves(c, down, own_ref, other_ref, 1024)


def grads_mlp0(normed, d_up, act, cot, after):
    tokens, width = normed.shape[1:]
    part = pl.BlockSpec((1, tokens, 256), lambda i: (0, 0, i))
    whole = pl.BlockSpec(d_up.shape, lambda i: (0, 0, 0), pipeline_mode=pl.Buffered(1))
    return pl.pallas_call(
        grads_mlp0_kernel,
        grid=(width // 256,),
        in_specs=[part, whole, part, whole] + [ANY] * len(after),
        out_specs=pl.BlockSpec((256, 2048), lambda i: (i, 0)),
        out_shape=jax.ShapeDtypeStruct((width, 2048), BF),
        compiler_params=pltpu.CompilerParams(vmem_limit_bytes=24 * MB),
        cost_estimate=QUICK,
        name="grads_mlp0",
    )(normed, d_up, act, cot, *after)


def grads_mlp1(c, normed, d_up, act, cot, first):
    tokens, width = normed.shape[1:]
    part = pl.BlockSpec((1, tokens, 256), lambda i, c: (0, 0, i))
    whole = pl.BlockSpec(d_up.shape, lambda i, c: (0, 0, 0), pipeline_mode=pl.Buffered(1))
    return pl.pallas_call(
        grads_mlp1_kernel,
        grid_spec=pltpu.PrefetchScalarGridSpec(
            num_scalar_prefetch=1,
            grid=(width // 256,),
            in_specs=[part, whole, part, whole, pl.BlockSpec((256, 2048), lambda i, c: (i, 0))],
            out_specs=[pl.BlockSpec((128, 2048), lambda i, c: (i, 0))] * 2,
        ),
        out_shape=[jax.ShapeDtypeStruct((width // 2, 2048), BF)] * 2,
        compiler_params=pltpu.CompilerParams(vmem_limit_bytes=46 * MB),
        cost_estimate=QUICK,
        name="grads_mlp1",
    )(c, normed, d_up, act, cot, first)


def grads_att_kernel(
    c_ref, n0_ref, n1_ref, dqkv0_ref, dqkv1_ref, mix0_ref, mix1_ref, cot0_ref, cot1_ref,
    *rest,
):
    own_ref, other_ref, out_s = rest[-3:]
    c = c_ref[0]
    i = pl.program_id(0)

    @pl.when(i == 0)
    def _():
        out_s[...] = dot_tn(mix0_ref[0], cot0_ref[0]) + dot_tn(mix1_ref[0], cot1_ref[0])

    for part in range(3):
        both = dot_tn(n0_ref[0], dqkv0_ref[0, part]) + dot_tn(n1_ref[0], dqkv1_ref[0, part])
        put_halves(c, both, own_ref, other_ref, part * 256)
    rows = out_s[pl.ds(pl.multiple_of(i * 64, 64), 64), :]
    rows = [rows[d * 8 : d * 8 + 8, b * 256 : b * 256 + 256] for d in range(8) for b in range(4)]
    put_halves(c, jnp.concatenate(rows), own_ref, other_ref, 768)


def grads_att(c, normed, d_qkv, mixed, cot, after):
    tokens, width = normed[0].shape[1:]

    def whole(a):
        return pl.BlockSpec(a.shape, lambda i, c: (0,) * a.ndim, pipeline_mode=pl.Buffered(1))

    return pl.pallas_call(
        grads_att_kernel,
        grid_spec=pltpu.PrefetchScalarGridSpec(
            num_scalar_prefetch=1,
            grid=(4,),
            in_specs=[pl.BlockSpec((1, tokens, 256), lambda i, c: (0, 0, i))] * 2
            + [whole(a) for a in (*d_qkv, *mixed, *cot)]
            + [ANY] * len(after),
            out_specs=[pl.BlockSpec((128, 1024), lambda i, c: (i, 0))] * 2,
            scratch_shapes=[pltpu.VMEM((256, 1024), F32)],
        ),
        out_shape=[jax.ShapeDtypeStruct((512, 1024), BF)] * 2,
        compiler_params=pltpu.CompilerParams(vmem_limit_bytes=58 * MB),
        cost_estimate=QUICK,
        name="grads_att",
    )(c, *normed, *d_qkv, *mixed, *cot, *after)


def finish_kernel(x_ref, c_ref, vec_ref, part_ref, *rest):
    out_ref, dx_ref = rest[-2:]
    x = x_ref[0, 0].astype(F32)
    branch, g = part_ref[0].astype(F32), part_ref[1].astype(F32)
    out_ref[0] = (x + (branch + vec_ref[4:5, :])).astype(BF)
    centered = x - jnp.mean(x, axis=-1, keepdims=True)
    rs = lax.rsqrt(jnp.mean(centered * centered, axis=-1, keepdims=True) + 1e-05)
    xhat = centered * rs
    g = g * vec_ref[0:1, :]
    mean_g = jnp.mean(g, axis=-1, keepdims=True)
    mean_gx = jnp.mean(g * xhat, axis=-1, keepdims=True)
    dx_ref[0] = c_ref[0, 0].astype(F32) + rs * (g - mean_g - xhat * mean_gx)


def finish(micro, x, cot, part, vectors, others, after=()):
    n, d = x.shape[2:]
    tile = pl.BlockSpec((1, 1, 128, d), lambda i: (micro, 0, i, 0))
    out = pl.BlockSpec((1, 128, d), lambda i: (micro, i, 0))
    return pl.pallas_call(
        finish_kernel,
        grid=(n // 128,),
        in_specs=[tile] * 2
        + [
            pl.BlockSpec((8, d), lambda i: (0, 0)),
            pl.BlockSpec((2, 128, d), lambda i: (0, i, 0)),
        ]
        + [ANY] * (len(others) + len(after)),
        out_specs=[out] * 2,
        out_shape=[jax.ShapeDtypeStruct((2, n, d), BF), jax.ShapeDtypeStruct((2, n, d), F32)],
        input_output_aliases={4 + k: k for k in range(len(others))},
        compiler_params=pltpu.CompilerParams(vmem_limit_bytes=58 * MB),
        cost_estimate=QUICK,
        name="finish",
    )(x, cot, vectors, part.reshape(2, n, d), *others, *after)


def add_kernel(a_ref, b_ref, *rest):
    rest[-1][...] = (a_ref[...].astype(F32) + b_ref[...].astype(F32)).astype(BF)


def add_after(a, b, after):
    n, d = a.shape
    part = pl.BlockSpec((n // 4, d), lambda i: (i, 0))
    return pl.pallas_call(
        add_kernel,
        grid=(4,),
        in_specs=[part, part] + [ANY] * len(after),
        out_specs=part,
        out_shape=jax.ShapeDtypeStruct((n, d), BF),
        compiler_params=pltpu.CompilerParams(vmem_limit_bytes=32 * MB),
        cost_estimate=QUICK,
        name="add_after",
    )(a, b, *after)


def to_columns_kernel(z_ref, up_ref, qkv_ref, down_ref, out_ref, *rest):
    vectors, rows_ref, pieces = rest[:6], rest[6], rest[7:]
    lines = [v[...].astype(F32).reshape(1, -1) for v in vectors]
    lines = [jnp.concatenate([v, jnp.zeros((1, 128 - v.shape[1]), F32)], axis=1) for v in lines]
    block = jnp.concatenate(lines + [jnp.zeros((2, 128), F32)], axis=0).astype(BF)
    for k, piece in enumerate(pieces):
        to = lax.rem(z_ref[0] + k, NZ)
        piece[:, 0:1024] = up_ref[:, pl.ds(pl.multiple_of(to * 1024, 1024), 1024)]
        for part in range(3):
            first = pl.multiple_of(part * 1024 + to * 256, 256)
            at = 1024 + part * 256
            piece[:, at : at + 256] = qkv_ref[:, pl.ds(first, 256)]
        piece[:, 1792:1920] = block
    rows_ref[0:32, :] = down_ref[...].astype(F32).astype(BF)
    rows_ref[32:40, :] = out_ref[...].astype(F32).astype(BF)


def to_payload_kernel(z_ref, g0_ref, g1_ref, g2_ref, g3_ref, rows_ref, after_ref, out_ref):
    got = [g[...].astype(F32) for g in (g0_ref, g1_ref, g2_ref, g3_ref)]
    columns = []
    for source in range(NZ):
        k = lax.rem(z_ref[0] - source + NZ, NZ)
        value = got[3]
        for j in range(3):
            value = jnp.where(k == j, got[j], value)
        columns.append(value)
    columns = jnp.concatenate(columns, axis=0)
    rows = rows_ref[...].astype(F32)
    w_out = jnp.concatenate([rows[32:40, b * 256 : b * 256 + 256] for b in range(4)], axis=0)
    out_ref[:, 0:1792] = columns[:, 0:1792].astype(BF)
    out_ref[:, 1792:2816] = rows[0:32].astype(BF)
    out_ref[:, 2816:3072] = w_out.astype(BF)
    out_ref[:, 3072:3200] = columns[:, 1792:1920].astype(BF)


def total_of(refs, rows):
    return sum([r[rows, :].astype(F32) for r in refs[1:]], refs[0][rows, :].astype(F32))


def to_xy_kernel(c_ref, own_ref, got_ref, va_ref, vb_ref, out_ref):
    total = total_of((own_ref, got_ref), slice(None))
    out_ref[:, :, 0:1024] = total.astype(BF).reshape(16, 32, 1024)
    vec = (va_ref[...] + vb_ref[...]).reshape(16, 2, 32, 128)
    out_ref[:, :, 1024:1152] = jnp.where(c_ref[0] == 0, vec[:, 0], vec[:, 1]).astype(BF)


def to_y_kernel(at_ref, mlp_ref, *outs):
    for k, out in enumerate(outs):
        rows = pl.ds(pl.multiple_of(lax.rem(at_ref[0] + k, 4) * 32, 32), 32)
        out[...] = mlp_ref[rows, :]


def to_z_kernel(att_ref, a_ref, b_ref, c_ref, d_ref, home_ref, rows_ref):
    mlp = total_of((a_ref, b_ref, c_ref, d_ref), slice(0, 32))
    att = att_ref[0].astype(F32)
    for k in range(1, 16):
        att = att + att_ref[k].astype(F32)
    home = jnp.concatenate([mlp[:, :1024], att[:, :768], att[:, 1024:1152]], axis=1)
    home_ref[...] = home.reshape(4, 8, 1920).astype(BF)
    rows_ref[0:32, :] = mlp[:, 1024:2048]
    out = att[:, 768:1024].reshape(4, 8, 256)
    for b in range(4):
        rows_ref[32:40, b * 256 : b * 256 + 256] = out[b]


def home_kernel(home_ref, up_ref, qkv_ref, *vectors):
    for k in range(NZ):
        up_ref[:, k * 1024 : k * 1024 + 1024] = home_ref[k, :, 0:1024].astype(F32)
        for part in range(3):
            at = part * 1024 + k * 256
            own = 1024 + part * 256
            qkv_ref[:, at : at + 256] = home_ref[k, :, own : own + 256].astype(F32)
    total = jnp.sum(home_ref[:, :, 1792:1920].astype(F32), axis=0)
    for k, ref in enumerate(vectors):
        ref[...] = total[k, : ref.shape[0]]


def in_vmem(kernel, name, operands, shapes, scalars=None, after=(), limit=58):
    def whole(shape):
        return pl.BlockSpec(shape, lambda i: (0,) * len(shape))

    specs = [whole(a.shape) for a in operands] + [ANY] * len(after)
    operands = (*operands, *after)
    if scalars is not None:
        specs = [pl.BlockSpec(memory_space=pltpu.SMEM)] + specs
        operands = (scalars, *operands)
    return pl.pallas_call(
        kernel,
        grid=(1,),
        in_specs=specs,
        out_specs=[whole(s[0]) for s in shapes],
        out_shape=[jax.ShapeDtypeStruct(*s) for s in shapes],
        compiler_params=pltpu.CompilerParams(vmem_limit_bytes=limit * MB),
        cost_estimate=QUICK,
        name=name,
    )(*operands)


def pack_kernel(a_ref, b_ref, *rest):
    rest[-1][0] = a_ref[0, 0]
    rest[-1][1] = b_ref[0, 0]


def pack(micro, a, b, after):
    n, d = a.shape[2:]
    part = pl.BlockSpec((1, 1, n // 2, d), lambda i: (micro, 0, i, 0))
    return pl.pallas_call(
        pack_kernel,
        grid=(2,),
        in_specs=[part, part] + [ANY] * len(after),
        out_specs=pl.BlockSpec((2, n // 2, d), lambda i: (0, i, 0)),
        out_shape=jax.ShapeDtypeStruct((2, n, d), BF),
        compiler_params=pltpu.CompilerParams(vmem_limit_bytes=58 * MB),
        cost_estimate=QUICK,
        name="pack",
    )(a, b, *after).reshape(2 * n, d)


def doc_positions(seg_row):
    length = seg_row.shape[-1]
    token_index = jnp.arange(length, dtype=jnp.int32)
    previous = jnp.concatenate([seg_row[..., :1], seg_row[..., :-1]], axis=-1)
    starts = jnp.where((token_index == 0) | (seg_row != previous), token_index, 0)
    doc_start = lax.cummax(starts, axis=seg_row.ndim - 1)
    return token_index - doc_start


def rotary_tables(positions):
    dim = jnp.arange(128, dtype=jnp.int32) % HEAD_DIM
    frequency = 10000.0 ** (-(dim % (ROT // 2)).astype(F32) * 2.0 / ROT)
    frequency = jnp.where(dim < ROT, frequency, 0.0)
    angles = positions.astype(F32)[..., None] * frequency
    return jnp.cos(angles), jnp.sin(angles) * jnp.where(dim < ROT // 2, -1.0, 1.0)


def send(value, axis, step):
    size = lax.axis_size(axis)
    return lax.ppermute(value, axis, [(i, (i + step) % size) for i in range(size)])


def exchange(parts, axis):
    return [parts[0]] + [send(parts[k], axis, k) for k in range(1, 4)]


def body(
    hidden_in,
    segments,
    valid_mask,
    w_qkv,
    w_out,
    w_up,
    w_down,
    b_qkv,
    b_out,
    b_up,
    b_down,
    ln_gain,
    ln_shift,
    cotangent,
):
    z = lax.axis_index("z")
    c = lax.axis_index("c").astype(jnp.int32).reshape(1)
    micro_count, _, group, width = hidden_in.shape
    row_len = group * NZ
    z_arr = z.astype(jnp.int32).reshape(1)

    w_rows, *columns = in_vmem(
        to_columns_kernel,
        "to_columns",
        (w_up, w_qkv, w_down, w_out, b_qkv, b_out, b_up, b_down, ln_gain, ln_shift),
        [((40, 1024), BF)] + [((8, 1920), BF)] * 4,
        z_arr,
    )
    there, back_home = [], []
    for d in range(32):
        for s in range(4):
            pair = (d * 4 + s, ((d % 8) * 4 + s) * 4 + d // 8)
            there.append(pair)
            back_home.append(pair[::-1])
    columns = exchange(columns, "z")
    w_rows = lax.ppermute(w_rows, ("x", "y", "c", "z"), there)
    mine0 = pack(0, hidden_in, cotangent, ())
    (payload,) = in_vmem(
        to_payload_kernel,
        "to_payload",
        (*columns, w_rows),
        [((32, 3200), BF)],
        z_arr,
        after=(mine0,),
    )
    weights = lax.all_gather(payload, ("x", "y", "c"), axis=0, tiled=True)

    pieces0 = [mine0] + [send(mine0, "z", -step) for step in range(1, NZ)]
    mine1 = pack(1, hidden_in, cotangent, (pieces0[2],))
    pieces1 = [mine1] + [send(mine1, "z", -step) for step in range(1, NZ)]

    seg = segments[:, 0]
    key_seg = jnp.where(valid_mask[:, 0] > 0, seg, -1)
    seg_row, seg_key = [
        jnp.broadcast_to(s.astype(F32)[:, None, :], (micro_count, 8, row_len)) for s in (seg, key_seg)
    ]
    tables = rotary_tables(doc_positions(seg))

    tables = [[t[m : m + 1] for t in tables] for m in range(micro_count)]

    lines = [[s[m : m + 1] for s in (seg_row, seg_key)] for m in range(micro_count)]

    def run_attend(m, heads, after, limit):
        return attend(z_arr, *heads, *lines[m], *tables[m], after, limit)

    hid0, cot0, n0, act0, dup0, *heads0, stat0, bup0, w_o, vecs = front(
        z_arr, pieces0, weights, (), *tables[0], (*lines[0], *lines[1]), 34
    )
    mix0, dqkv0, bqkv0 = run_attend(0, heads0, (), 30)
    first = grads_mlp0(n0, dup0, act0, cot0, (mix0,))
    cuts0, gain0, shift0 = back(
        z_arr, act0, mix0, dup0, dqkv0, hid0, stat0, weights, w_o, (first, *pieces1[1:]), 46
    )
    sum0 = lax.psum_scatter(cuts0, "z", scatter_dimension=0, tiled=True)
    hid1, cot1, n1, act1, dup1, *heads1, stat1, bup1 = front(
        z_arr, pieces1, weights, (w_o, vecs), *tables[1], (cuts0,), 48
    )
    cot = (cot0, cot1)
    mlp = grads_mlp1(c, n1, dup1, act1, cot1, first)
    mix1, dqkv1, bqkv1 = run_attend(1, heads1, (mlp[0],), 46)
    mlp = add_after(mlp[0], send(mlp[1], "c", 1), (mix1,))
    att = grads_att(c, (n0, n1), (dqkv0, dqkv1), (mix0, mix1), cot, (mlp,))
    mlp = lax.psum_scatter(mlp, "x", scatter_dimension=0, tiled=True)
    cuts1, gain1, shift1 = back(
        z_arr, act1, mix1, dup1, dqkv1, hid1, stat1, weights, w_o, (sum0, att[0]), 58
    )
    sum1 = lax.psum_scatter(cuts1, "z", scatter_dimension=0, tiled=True)
    sums = ((bqkv0, gain0, shift0), (bqkv1, gain1, shift1))
    sum_bup = bup0 + bup1
    sum_bqkv, sum_gain, sum_shift = [jnp.sum(a + b, axis=-2) for a, b in zip(*sums)]

    mine = jnp.arange(NZ) == z
    sum_cot = jnp.sum(cotangent.astype(F32), axis=(0, 1, 2)).reshape(128, 8)
    sum_bqkv = jnp.where(mine[None, :, None], sum_bqkv.reshape(3, 1, 256), 0.0)
    sum_bup = jnp.where(mine[:, None], jnp.sum(sum_bup, axis=0)[None, :], 0.0)
    parts = (
        sum_bqkv.reshape(128, 24),
        sum_cot,
        sum_bup.reshape(128, 32),
        sum_cot,
        sum_gain.reshape(128, 8),
        sum_shift.reshape(128, 8),
    )
    vec_grads = jnp.stack(
        [jnp.pad(p, ((0, 0), (0, 128 - p.shape[1]))) for p in parts] + [jnp.zeros((128, 128), F32)] * 2,
        axis=1,
    ).reshape(1024, 128)
    mlp = in_vmem(
        to_y_kernel,
        "to_y",
        (mlp,),
        [((32, 2048), BF)] * 4,
        lax.axis_index("y").astype(jnp.int32).reshape(1),
    )
    mlp = exchange(mlp, "y")
    (att,) = in_vmem(
        to_xy_kernel,
        "to_xy",
        (att[0], send(att[1], "c", 1), vec_grads, send(vec_grads, "c", 1)),
        [((16, 32, 1152), BF)],
        c,
        limit=32,
    )
    att = lax.all_to_all(att, ("x", "y"), 0, 0, tiled=True)
    home, rows_home = in_vmem(
        to_z_kernel,
        "to_z",
        (att, *mlp),
        [((4, 8, 1920), BF), ((40, 1024), F32)],
    )
    home = lax.all_to_all(home, "z", 0, 0, tiled=True)
    rows_home = lax.ppermute(rows_home, ("x", "y", "c", "z"), back_home)
    final_up, final_qkv, *final_vectors = in_vmem(
        home_kernel,
        "home",
        (home,),
        [((8, 4096), F32), ((8, 3072), F32)] + [((n,), F32) for n in (24, 8, 32, 8, 8, 8)],
    )
    half = finish(0, hidden_in, cotangent, sum0, vecs, ())
    out_hidden, grad_input = finish(1, hidden_in, cotangent, sum1, vecs, half, (final_up,))
    out_hidden, grad_input = out_hidden[:, None], grad_input[:, None]
    return (
        out_hidden,
        grad_input,
        final_qkv,
        rows_home[32:],
        final_up,
        rows_home[:32],
        *final_vectors,
    )


def solution(mesh):
    parts = jax.sharding.Mesh(mesh.devices.reshape(4, 4, 2, NZ), ("x", "y", "c", "z"))
    dp = ("x", "y", "c")
    rows = P(None, dp, "z", None)
    tokens = P(None, dp, None)
    matrix = P(dp + ("z",), None)
    vector = P(dp + ("z",))
    in_specs = (rows, tokens, tokens) + (matrix,) * 4 + (vector,) * 6 + (rows,)
    out_specs = (rows, rows) + (matrix,) * 4 + (vector,) * 6
    return jax.shard_map(body, mesh=parts, in_specs=in_specs, out_specs=out_specs, check_vma=False)
```

profile of v0, /device:TPU:0, one launch (start us, length us, event | category | flops | bytes accessed | tf_op | source)
XLA Modules:
  0.0 286.3 jit_solution(13456958328404055751)
XLA Ops:
  7.2 1.6 to_columns.1
  8.9 1.5 collective-permute-start.6
  10.4 2.5 collective-permute-start.3
  12.9 3.6 %collective-permute-start.4 = (bf16[8,1920]{1,0:T(8,128)(2,1)}, bf16[8,1920]{1,0:T(8,128)(2,1)S(1)}, u32[]{:S(2)}, u32[]{:S(2)}) collective-permute-start(bf16[8,1920]{1,0:T(8,128)(2,1)} %get-tuple-element.77), channel_id=1, source_target_pairs={{0,2},{1,3},{2,0},{3,1},{4,6},{5,7},{6,4},{7,5},{8,10},{9,11},{10,... | collective-permute-start | bytes 92168 | tf_op jit(solution)/shard_map/ppermute | solution.py:684
  16.5 1.7 collective-permute-start.5
  18.1 2.0 pack.2
  21.4 1.7 to_payload.1
  23.1 2.7 collective-permute-start.1
  25.9 1.1 collective-permute-start
  27.0 0.9 collective-permute-start.2
  29.1 21.8 %collective-permute-done.1.rest_2_.rest_0_ = bf16[512,1024]{1,0:T(8,128)(2,1)S(1)} collective-permute-done((bf16[512,1024]{1,0:T(8,128)(2,1)}, bf16[512,1024]{1,0:T(8,128)(2,1)S(1)}, u32[]{:S(2)}, u32[]{:S(2)}) %collective-permute-start.1) | collective-permute-done | bytes 1048608 | tf_op jit(solution)/shard_map/ppermute | solution.py:684
  51.0 1.1 copy-done.18
  52.0 2.1 pack.3
  54.1 3.7 %collective-permute-start.7 = (bf16[512,1024]{1,0:T(8,128)(2,1)}, bf16[512,1024]{1,0:T(8,128)(2,1)}, u32[]{:S(2)}, u32[]{:S(2)}) collective-permute-start(bf16[512,1024]{1,0:T(8,128)(2,1)} %bitcast.58), channel_id=1, source_target_pairs={{0,3},{1,0},{2,1},{3,2},{4,7},{5,4},{6,5},{7,6},{8,11},{9,8},{10,9... | collective-permute-start | bytes 3145736 | tf_op jit(solution)/shard_map/ppermute | solution.py:684
  57.8 0.9 collective-permute-start.9
  58.7 3.7 %fusion = (f32[2,1024,128]{2,1,0:T(8,128)S(1)}, f32[2,1024,128]{2,1,0:T(8,128)S(1)}) fusion(f32[128]{0:T(128)S(1)} %compare_select_fusion.3, f32[128]{0:T(128)S(1)} %compare_select_fusion.4, f32[2,1024]{1,0:T(2,128)S(1)} %fusion.2), kind=kLoop, calls=%fused_computation.3 | loop fusion | flops 524288 | bytes 2106368 | tf_op jit(solution)/shard_map/mul | solution.py:679
  62.4 1.4 fusion.10
  63.8 10.6 %collective-permute-done.rest_1_ = bf16[512,1024]{1,0:T(8,128)(2,1)S(1)} collective-permute-done((bf16[512,1024]{1,0:T(8,128)(2,1)}, bf16[512,1024]{1,0:T(8,128)(2,1)S(1)}, u32[]{:S(2)}, u32[]{:S(2)}) %collective-permute-start) | collective-permute-done | bytes 1048608 | tf_op jit(solution)/shard_map/ppermute | solution.py:684
  74.4 1.0 copy-done.22
  75.4 1.0 copy-done.24
  76.4 1.0 copy-done.13
  77.5 1.0 copy-done.14
  78.5 1.2 copy-done.19
  79.7 1.2 copy-done.23
  81.0 1.2 copy-done.25
  82.2 13.8 %front.2 = (bf16[1,1024,1024]{2,1,0:T(8,128)(2,1)S(1)}, bf16[1,1024,1024]{2,1,0:T(8,128)(2,1)S(1)}, bf16[1,1024,1024]{2,1,0:T(8,128)(2,1)S(1)}, bf16[1,1024,1024...) custom-call(s32[1]{0:T(128)} %bitcast.z_ref, ...), custom_call_target="tpu_custom_call" | custom-call | flops 1024 | bytes 1024 | tf_op jit(solution)/shard_map/front/pallas_call | solution.py:200
  96.1 1.4 copy-done.21
  97.4 13.3 %attend.2 = (bf16[1,1024,256]{2,1,0:T(8,128)(2,1)S(1)}, bf16[1,3,1024,256]{3,2,1,0:T(8,128)(2,1)S(1)}, f32[3,8,256]{2,1,0:T(8,128)S(1)}) custom-call(s32[1]{0:T(128)} %bitcast.z_ref, bf16[1,1024,256]{2,1,0:T(8,128)(2,1)S(1)} %get-tuple-element.83.q_ref, bf16[1,1024,256]{2,1,0:T(8,128)(2,1)S(1)} %get-tuple-element.84.k_ref, ...), custom_call_target="tpu_custom_call" | custom-call | flops 1024 | bytes 1024 | tf_op jit(solution)/shard_map/attend/pallas_call | solution.py:312
  110.8 5.7 %grads_mlp0.1.rest_0_.sum_ref = bf16[1024,2048]{1,0:T(8,128)(2,1)S(1)} custom-call(bf16[1,1024,1024]{2,1,0:T(8,128)(2,1)S(1)} %get-tuple-element.92.n_ref.n0_ref, bf16[1,1024,1024]{2,1,0:T(8,128)(2,1)S(1)} %get-tuple-element.88.dup_ref, bf16[1,1024,1024]{2,1,0:T(8,128)(2,1)S(1)} %get-tuple-element.82.act_ref, ...), custom_call_target="tpu_custom_call" | custom-call | flops 1024 | bytes 1024 | tf_op jit(solution)/shard_map/grads_mlp0/pallas_call | solution.py:417
  116.5 2.0 copy-done
  118.6 24.4 %back.2 = (bf16[2048,1024]{1,0:T(8,128)(2,1)}, f32[8,1024]{1,0:T(8,128)S(1)}, f32[8,1024]{1,0:T(8,128)S(1)}) custom-call(s32[1]{0:T(128)} %bitcast.z_ref, bf16[1,1024,1024]{2,1,0:T(8,128)(2,1)} %copy-done.2, bf16[1,1024,256]{2,1,0:T(8,128)(2,1)S(1)} %get-tuple-element.87.rest_0_.mix_ref.mix0_ref, bf16[1,1024,1024]{2,1,0:T(8,128)(2,1)} %copy-done.3, ...), custom_call_target="tpu_custom_call" | custom-call | flops 1024 | bytes 1024 | tf_op jit(solution)/shard_map/back/pallas_call | solution.py:368
  143.2 0.9 copy-done.10
  144.8 15.1 %front.3 = (bf16[1,1024,1024]{2,1,0:T(8,128)(2,1)}, bf16[1,1024,1024]{2,1,0:T(8,128)(2,1)}, bf16[1,1024,1024]{2,1,0:T(8,128)(2,1)}, bf16[1,1024,1024]{2,1,0:T(8,...) custom-call(s32[1]{0:T(128)} %bitcast.z_ref, ...), custom_call_target="tpu_custom_call" | custom-call | flops 1024 | bytes 1024 | tf_op jit(solution)/shard_map/front/pallas_call | solution.py:200
  159.8 1.8 copy-done.6
  161.7 8.5 %grads_mlp1.1 = (bf16[512,2048]{1,0:T(8,128)(2,1)S(1)}, bf16[512,2048]{1,0:T(8,128)(2,1)S(1)}) custom-call(s32[1]{0:T(128)} %bitcast.8.c_ref, bf16[1,1024,1024]{2,1,0:T(8,128)(2,1)S(1)} %copy-done.6, bf16[1,1024,1024]{2,1,0:T(8,128)(2,1)} %get-tuple-element.101.dup_ref, bf16[1,1024,1024]{2,1,0:T(8,128)(2,1)} %get-tuple-element.95.act_ref, ...), custom_call_target="tpu_custom_call" | custom-call | flops 1024 | bytes 1024 | tf_op jit(solution)/shard_map/grads_mlp1/pallas_call | solution.py:433
  170.3 13.3 %attend.3 = (bf16[1,1024,256]{2,1,0:T(8,128)(2,1)S(1)}, bf16[1,3,1024,256]{3,2,1,0:T(8,128)(2,1)S(1)}, f32[3,8,256]{2,1,0:T(8,128)S(1)}) custom-call(s32[1]{0:T(128)} %bitcast.z_ref, bf16[1,1024,256]{2,1,0:T(8,128)(2,1)S(1)} %get-tuple-element.96.q_ref, bf16[1,1024,256]{2,1,0:T(8,128)(2,1)S(1)} %get-tuple-element.97.k_ref, ...), custom_call_target="tpu_custom_call" | custom-call | flops 1024 | bytes 1024 | tf_op jit(solution)/shard_map/attend/pallas_call | solution.py:312
  183.6 1.1 copy-done.8
  184.7 2.1 add_after.1.rest_0_
  186.9 10.6 %grads_att.1 = (bf16[512,1024]{1,0:T(8,128)(2,1)}, bf16[512,1024]{1,0:T(8,128)(2,1)}) custom-call(s32[1]{0:T(128)} %bitcast.8.c_ref, bf16[1,1024,1024]{2,1,0:T(8,128)(2,1)} %copy-done.5, bf16[1,1024,1024]{2,1,0:T(8,128)(2,1)} %get-tuple-element.100.n_ref.n1_ref, bf16[1,3,1024,256]{3,2,1,0:T(8,128)(2,1)} %copy-done.7, bf16[1,3,1024,256]{3,2,1,0:T(8,128)(2,1)} %copy-done.8, ...), custom_call_target="tpu_custom_call" | custom-call | flops 1024 | bytes 1024 | tf_op jit(solution)/shard_map/grads_att/pallas_call | solution.py:474
  197.5 12.9 %back.3 = (bf16[2048,1024]{1,0:T(8,128)(2,1)}, f32[8,1024]{1,0:T(8,128)}, f32[8,1024]{1,0:T(8,128)}) custom-call(s32[1]{0:T(128)} %bitcast.z_ref, bf16[1,1024,1024]{2,1,0:T(8,128)(2,1)} %get-tuple-element.95.act_ref, bf16[1,1024,256]{2,1,0:T(8,128)(2,1)} %copy-done.12, bf16[1,1024,1024]{2,1,0:T(8,128)(2,1)} %get-tuple-element.101.dup_ref, ...), custom_call_target="tpu_custom_call" | custom-call | flops 1024 | bytes 1024 | tf_op jit(solution)/shard_map/back/pallas_call | solution.py:368
  210.7 1.0 copy-done.28
  213.3 0.7 stack.28
  214.2 1.1 collective-permute-done.11.got_ref
  215.3 0.8 collective-permute-done.12.vb_ref
  216.0 1.3 to_xy.1
  217.3 7.6 %all-to-all-start = ((bf16[16,32,1152]{2,1,0:T(8,128)(2,1)}), bf16[16,32,1152]{2,1,0:T(8,128)(2,1)S(1)}, u32[]{:S(2)}, u32[]{:S(2)}) async-start(bf16[16,32,1152]{2,1,0:T(8,128)(2,1)} %to_xy.1), calls=%async_computation.2 | async-start | bytes 2359296 | tf_op jit(solution)/shard_map/all_to_all | solution.py:815
  225.0 1.8 to_y.1
  226.8 1.9 collective-permute-start.13
  228.7 2.7 collective-permute-start.14
  231.4 1.5 collective-permute-start.15
  232.9 11.0 %collective-permute-done.13.b_ref = bf16[32,2048]{1,0:T(8,128)(2,1)S(1)} collective-permute-done((bf16[32,2048]{1,0:T(8,128)(2,1)}, bf16[32,2048]{1,0:T(8,128)(2,1)S(1)}, u32[]{:S(2)}, u32[]{:S(2)}) %collective-permute-start.13) | collective-permute-done | bytes 131104 | tf_op jit(solution)/shard_map/ppermute | solution.py:684
  243.9 3.4 %collective-permute-done.14.c_ref = bf16[32,2048]{1,0:T(8,128)(2,1)S(1)} collective-permute-done((bf16[32,2048]{1,0:T(8,128)(2,1)}, bf16[32,2048]{1,0:T(8,128)(2,1)S(1)}, u32[]{:S(2)}, u32[]{:S(2)}) %collective-permute-start.14) | collective-permute-done | bytes 131104 | tf_op jit(solution)/shard_map/ppermute | solution.py:684
  247.3 0.6 copy-done.32
  248.4 2.3 to_z.1
  250.7 1.6 collective-permute-start.16
  252.3 7.6 %all-to-all-start.1 = ((bf16[4,8,1920]{2,1,0:T(8,128)(2,1)}), bf16[4,8,1920]{2,1,0:T(8,128)(2,1)S(1)}, u32[]{:S(2)}, u32[]{:S(2)}) async-start(bf16[4,8,1920]{2,1,0:T(8,128)(2,1)} %get-tuple-element.126), calls=%async_computation.4 | async-start | bytes 245760 | tf_op jit(solution)/shard_map/all_to_all | solution.py:822
  259.8 2.8 finish.2
  262.7 4.8 %all-to-all-done.1.home_ref = bf16[4,8,1920]{2,1,0:T(8,128)(2,1)S(1)} async-done(((bf16[4,8,1920]{2,1,0:T(8,128)(2,1)}), bf16[4,8,1920]{2,1,0:T(8,128)(2,1)S(1)}, u32[]{:S(2)}, u32[]{:S(2)}) %all-to-all-start.1) | async-done | bytes 122912 | tf_op jit(solution)/shard_map/all_to_all | solution.py:822
  267.4 0.6 copy-done.30
  268.1 1.6 home.1
  269.7 0.7 slice.88
  270.4 0.6 slice.87
  271.0 5.7 %reduce-scatter.6.cloned.1.call-done = bf16[512,1024]{1,0:T(8,128)(2,1)} async-done(((bf16[2048,1024]{1,0:T(8,128)(2,1)}), bf16[512,1024]{1,0:T(8,128)(2,1)}) %reduce-scatter.6.cloned.1.call-update) | async-done | bytes 1048592 | tf_op jit(solution)/shard_map/reduce_scatter | solution.py:778
  276.7 2.8 finish.3
  (135 shorter events, 5.7 us)
Async XLA Ops:
  7.2 69.2 %all-gather.2.cloned.1.call-start = ((), (), s32[]{:S(2)}) async-start(), calls=%async_computation.5 | async-start | bytes 6758400 | tf_op jit(solution)/shard_map/all_gather | solution.py:737
  8.9 11.8 %collective-permute-start.6 = (bf16[40,1024]{1,0:T(8,128)(2,1)}, bf16[40,1024]{1,0:T(8,128)(2,1)S(1)}, u32[]{:S(2)}, u32[]{:S(2)}) collective-permute-start(bf16[40,1024]{1,0:T(8,128)(2,1)} %get-tuple-element.79), channel_id=1, source_target_pairs={{0,0},{1,4},{2,8},{3,12},{4,16},{5,20},{6,24},{7,28},{8,32},{9,36}... | collective-permute-start | bytes 245768 | tf_op jit(solution)/shard_map/ppermute | solution.py:727
  10.4 9.7 %collective-permute-start.3 = (bf16[8,1920]{1,0:T(8,128)(2,1)}, bf16[8,1920]{1,0:T(8,128)(2,1)S(1)}, u32[]{:S(2)}, u32[]{:S(2)}) collective-permute-start(bf16[8,1920]{1,0:T(8,128)(2,1)} %get-tuple-element.76), channel_id=1, source_target_pairs={{0,1},{1,2},{2,3},{3,0},{4,5},{5,6},{6,7},{7,4},{8,9},{9,10},{10,1... | collective-permute-start | bytes 92168 | tf_op jit(solution)/shard_map/ppermute | solution.py:684
  12.9 7.3 %collective-permute-start.4 = (bf16[8,1920]{1,0:T(8,128)(2,1)}, bf16[8,1920]{1,0:T(8,128)(2,1)S(1)}, u32[]{:S(2)}, u32[]{:S(2)}) collective-permute-start(bf16[8,1920]{1,0:T(8,128)(2,1)} %get-tuple-element.77), channel_id=1, source_target_pairs={{0,2},{1,3},{2,0},{3,1},{4,6},{5,7},{6,4},{7,5},{8,10},{9,11},{10,... | collective-permute-start | bytes 92168 | tf_op jit(solution)/shard_map/ppermute | solution.py:684
  16.4 11.5 %copy-start.35 = (s32[2,1,1024]{2,1,0:T(1,128)S(1)}, s32[2,1,1024]{2,1,0:T(1,128)}, u32[]{:S(2)}) copy-start(s32[2,1,1024]{2,1,0:T(1,128)} %param.15) | copy-start | bytes 24580
  16.5 4.3 %collective-permute-start.5 = (bf16[8,1920]{1,0:T(8,128)(2,1)}, bf16[8,1920]{1,0:T(8,128)(2,1)S(1)}, u32[]{:S(2)}, u32[]{:S(2)}) collective-permute-start(bf16[8,1920]{1,0:T(8,128)(2,1)} %get-tuple-element.78), channel_id=1, source_target_pairs={{0,3},{1,0},{2,1},{3,2},{4,7},{5,4},{6,5},{7,6},{8,11},{9,8},{10,9... | collective-permute-start | bytes 92168 | tf_op jit(solution)/shard_map/ppermute | solution.py:684
  20.1 0.6 copy-start.38
  20.2 0.6 copy-start.39
  20.7 0.6 copy-start.34
  23.1 174.5 %reduce-scatter.4.cloned.1.call-start = ((), (), s32[]{:S(2)}) async-start(), calls=%async_computation.6 | async-start | bytes 5242880 | tf_op jit(solution)/shard_map/reduce_scatter | solution.py:765
  23.1 27.8 %collective-permute-start.1 = (bf16[512,1024]{1,0:T(8,128)(2,1)}, bf16[512,1024]{1,0:T(8,128)(2,1)S(1)}, u32[]{:S(2)}, u32[]{:S(2)}) collective-permute-start(bf16[512,1024]{1,0:T(8,128)(2,1)} %bitcast.54), channel_id=1, source_target_pairs={{0,2},{1,3},{2,0},{3,1},{4,6},{5,7},{6,4},{7,5},{8,10},{9,11},{10,... | collective-permute-start | bytes 3145736 | tf_op jit(solution)/shard_map/ppermute | solution.py:684
  25.9 48.6 %collective-permute-start = (bf16[512,1024]{1,0:T(8,128)(2,1)}, bf16[512,1024]{1,0:T(8,128)(2,1)S(1)}, u32[]{:S(2)}, u32[]{:S(2)}) collective-permute-start(bf16[512,1024]{1,0:T(8,128)(2,1)} %bitcast.55), channel_id=1, source_target_pairs={{0,3},{1,0},{2,1},{3,2},{4,7},{5,4},{6,5},{7,6},{8,11},{9,8},{10,9... | collective-permute-start | bytes 3145736 | tf_op jit(solution)/shard_map/ppermute | solution.py:684
  27.0 48.5 %collective-permute-start.2 = (bf16[512,1024]{1,0:T(8,128)(2,1)}, bf16[512,1024]{1,0:T(8,128)(2,1)S(1)}, u32[]{:S(2)}, u32[]{:S(2)}) collective-permute-start(bf16[512,1024]{1,0:T(8,128)(2,1)} %bitcast.56), channel_id=1, source_target_pairs={{0,1},{1,2},{2,3},{3,0},{4,5},{5,6},{6,7},{7,4},{8,9},{9,10},{10,1... | collective-permute-start | bytes 3145736 | tf_op jit(solution)/shard_map/ppermute | solution.py:684
  29.1 29.5 %copy-start.41 = (s32[2,1,1024]{2,1,0:T(1,128)S(1)}, s32[2,1,1024]{2,1,0:T(1,128)}, u32[]{:S(2)}) copy-start(s32[2,1,1024]{2,1,0:T(1,128)} %param.16) | copy-start | bytes 24580
  51.0 1.1 copy-start.18
  54.1 64.5 %collective-permute-start.7 = (bf16[512,1024]{1,0:T(8,128)(2,1)}, bf16[512,1024]{1,0:T(8,128)(2,1)}, u32[]{:S(2)}, u32[]{:S(2)}) collective-permute-start(bf16[512,1024]{1,0:T(8,128)(2,1)} %bitcast.58), channel_id=1, source_target_pairs={{0,3},{1,0},{2,1},{3,2},{4,7},{5,4},{6,5},{7,6},{8,11},{9,8},{10,9... | collective-permute-start | bytes 3145736 | tf_op jit(solution)/shard_map/ppermute | solution.py:684
  57.8 60.8 %collective-permute-start.8 = (bf16[512,1024]{1,0:T(8,128)(2,1)}, bf16[512,1024]{1,0:T(8,128)(2,1)}, u32[]{:S(2)}, u32[]{:S(2)}) collective-permute-start(bf16[512,1024]{1,0:T(8,128)(2,1)} %bitcast.59), channel_id=1, source_target_pairs={{0,2},{1,3},{2,0},{3,1},{4,6},{5,7},{6,4},{7,5},{8,10},{9,11},{10,... | collective-permute-start | bytes 3145736 | tf_op jit(solution)/shard_map/ppermute | solution.py:684
  57.8 60.8 %collective-permute-start.9 = (bf16[512,1024]{1,0:T(8,128)(2,1)}, bf16[512,1024]{1,0:T(8,128)(2,1)}, u32[]{:S(2)}, u32[]{:S(2)}) collective-permute-start(bf16[512,1024]{1,0:T(8,128)(2,1)} %bitcast.60), channel_id=1, source_target_pairs={{0,1},{1,2},{2,3},{3,0},{4,5},{5,6},{6,7},{7,4},{8,9},{9,10},{10,1... | collective-permute-start | bytes 3145736 | tf_op jit(solution)/shard_map/ppermute | solution.py:684
  62.4 14.0 %copy-start.1 = (bf16[2,256,1024]{2,1,0:T(8,128)(2,1)S(1)}, bf16[2,256,1024]{2,1,0:T(8,128)(2,1)}, u32[]{:S(2)}) copy-start(bf16[2,256,1024]{2,1,0:T(8,128)(2,1)} %pack.2) | copy-start | bytes 3145732
  74.4 1.0 copy-start.22
  75.4 1.0 copy-start.24
  76.4 1.0 copy-start.13
  77.5 1.0 copy-start.14
  78.5 1.2 copy-start.19
  79.7 1.2 copy-start.23
  81.0 1.2 copy-start.25
  96.0 1.4 copy-start.21
  97.4 19.1 %copy-start.2 = (bf16[1,1024,1024]{2,1,0:T(8,128)(2,1)}, bf16[1,1024,1024]{2,1,0:T(8,128)(2,1)S(1)}, u32[]{:S(2)}) copy-start(bf16[1,1024,1024]{2,1,0:T(8,128)(2,1)S(1)} %get-tuple-element.82.act_ref) | copy-start | bytes 6291460
  97.4 19.1 %copy-start.3 = (bf16[1,1024,1024]{2,1,0:T(8,128)(2,1)}, bf16[1,1024,1024]{2,1,0:T(8,128)(2,1)S(1)}, u32[]{:S(2)}) copy-start(bf16[1,1024,1024]{2,1,0:T(8,128)(2,1)S(1)} %get-tuple-element.88.dup_ref) | copy-start | bytes 6291460
  97.4 19.1 %copy-start.4 = (bf16[1,1024,1024]{2,1,0:T(8,128)(2,1)}, bf16[1,1024,1024]{2,1,0:T(8,128)(2,1)S(1)}, u32[]{:S(2)}) copy-start(bf16[1,1024,1024]{2,1,0:T(8,128)(2,1)S(1)} %get-tuple-element.93.cot_ref.cot0_ref) | copy-start | bytes 6291460
  97.4 19.1 %copy-start.5 = (bf16[1,1024,1024]{2,1,0:T(8,128)(2,1)}, bf16[1,1024,1024]{2,1,0:T(8,128)(2,1)S(1)}, u32[]{:S(2)}) copy-start(bf16[1,1024,1024]{2,1,0:T(8,128)(2,1)S(1)} %get-tuple-element.92.n_ref.n0_ref) | copy-start | bytes 6291460
  97.4 21.2 %copy-start.9 = (bf16[256,1024]{1,0:T(8,128)(2,1)}, bf16[256,1024]{1,0:T(8,128)(2,1)S(1)}, u32[]{:S(2)}) copy-start(bf16[256,1024]{1,0:T(8,128)(2,1)S(1)} %get-tuple-element.81.wo_ref.rest_5_) | copy-start | bytes 1572868
  97.4 45.7 %copy-start.27 = (f32[8,1024]{1,0:T(8,128)}, f32[8,1024]{1,0:T(8,128)S(1)}, u32[]{:S(2)}) copy-start(f32[8,1024]{1,0:T(8,128)S(1)} %get-tuple-element.80.rest_6_.vec_ref) | copy-start | bytes 98308
  110.7 7.9 %copy-start.7 = (bf16[1,3,1024,256]{3,2,1,0:T(8,128)(2,1)}, bf16[1,3,1024,256]{3,2,1,0:T(8,128)(2,1)S(1)}, u32[]{:S(2)}) copy-start(bf16[1,3,1024,256]{3,2,1,0:T(8,128)(2,1)S(1)} %get-tuple-element.89.dqkv_ref.dqkv0_ref) | copy-start | bytes 4718596
  110.7 7.9 %copy-start.11 = (bf16[1,1024,256]{2,1,0:T(8,128)(2,1)}, bf16[1,1024,256]{2,1,0:T(8,128)(2,1)S(1)}, u32[]{:S(2)}) copy-start(bf16[1,1024,256]{2,1,0:T(8,128)(2,1)S(1)} %get-tuple-element.87.rest_0_.mix_ref.mix0_ref) | copy-start | bytes 1572868
  116.5 2.0 copy-start
  143.0 1.0 copy-start.10
  143.1 1.2 copy-start.15
  143.1 1.4 copy-start.16
  143.1 1.7 copy-start.17
  143.1 81.9 %reduce-scatter.8.cloned.1.call-start = ((), (), s32[]{:S(2)}) async-start(), calls=%async_computation.8 | async-start | bytes 2621440 | tf_op jit(solution)/shard_map/reduce_scatter | solution.py:774
  159.8 10.3 %copy-start.26 = (f32[1,1024,128]{2,1,0:T(8,128)}, f32[1,1024,128]{2,1,0:T(8,128)S(1)}, u32[]{:S(2)}) copy-start(f32[1,1024,128]{2,1,0:T(8,128)S(1)} %get-tuple-element.107.stat_ref) | copy-start | bytes 1572868
  159.8 1.8 copy-start.6
  170.2 14.5 %collective-permute-start.10 = (bf16[512,2048]{1,0:T(8,128)(2,1)S(1)}, bf16[512,2048]{1,0:T(8,128)(2,1)S(1)}, u32[]{:S(2)}, u32[]{:S(2)}) collective-permute-start(bf16[512,2048]{1,0:T(8,128)(2,1)S(1)} %get-tuple-element.108), channel_id=1, source_target_pairs={{0,4},{4,0},{1,5},{5,1},{2,6},{6,2},{3,7},{7,3},{8,12},{12,8},{9,1... | collective-permute-start | bytes 6291464 | tf_op jit(solution)/shard_map/ppermute | solution.py:684
  183.5 1.1 copy-start.8
  184.7 2.1 copy-start.12
  186.9 89.8 %reduce-scatter.6.cloned.1.call-start = ((), (), s32[]{:S(2)}) async-start(), calls=%async_computation.7 | async-start | bytes 5242880 | tf_op jit(solution)/shard_map/reduce_scatter | solution.py:778
  210.5 1.2 copy-start.28
  210.5 2.5 copy-start.37
  210.5 2.6 copy-start.36
  210.5 5.5 %copy-start.20 = (bf16[512,1024]{1,0:T(8,128)(2,1)S(1)}, bf16[512,1024]{1,0:T(8,128)(2,1)}, u32[]{:S(2)}) copy-start(bf16[512,1024]{1,0:T(8,128)(2,1)} %get-tuple-element.109.rest_1_.own_ref) | copy-start | bytes 3145732
  212.2 3.1 %collective-permute-start.11 = (bf16[512,1024]{1,0:T(8,128)(2,1)}, bf16[512,1024]{1,0:T(8,128)(2,1)S(1)}, u32[]{:S(2)}, u32[]{:S(2)}) collective-permute-start(bf16[512,1024]{1,0:T(8,128)(2,1)} %get-tuple-element.113), channel_id=1, source_target_pairs={{0,4},{4,0},{1,5},{5,1},{2,6},{6,2},{3,7},{7,3},{8,12},{12,8},{9,1... | collective-permute-start | bytes 3145736 | tf_op jit(solution)/shard_map/ppermute | solution.py:684
  214.0 2.0 collective-permute-start.12
  217.3 30.0 %all-to-all-start = ((bf16[16,32,1152]{2,1,0:T(8,128)(2,1)}), bf16[16,32,1152]{2,1,0:T(8,128)(2,1)S(1)}, u32[]{:S(2)}, u32[]{:S(2)}) async-start(bf16[16,32,1152]{2,1,0:T(8,128)(2,1)} %to_xy.1), calls=%async_computation.2 | async-start | bytes 2359296 | tf_op jit(solution)/shard_map/all_to_all | solution.py:815
  226.8 17.1 %collective-permute-start.13 = (bf16[32,2048]{1,0:T(8,128)(2,1)}, bf16[32,2048]{1,0:T(8,128)(2,1)S(1)}, u32[]{:S(2)}, u32[]{:S(2)}) collective-permute-start(bf16[32,2048]{1,0:T(8,128)(2,1)} %get-tuple-element.123), channel_id=1, source_target_pairs={{0,8},{8,16},{16,24},{24,0},{1,9},{9,17},{17,25},{25,1},{2,10},{10... | collective-permute-start | bytes 393224 | tf_op jit(solution)/shard_map/ppermute | solution.py:684
  228.7 18.5 %collective-permute-start.14 = (bf16[32,2048]{1,0:T(8,128)(2,1)}, bf16[32,2048]{1,0:T(8,128)(2,1)S(1)}, u32[]{:S(2)}, u32[]{:S(2)}) collective-permute-start(bf16[32,2048]{1,0:T(8,128)(2,1)} %get-tuple-element.124), channel_id=1, source_target_pairs={{0,16},{8,24},{16,0},{24,8},{1,17},{9,25},{17,1},{25,9},{2,18},{10... | collective-permute-start | bytes 393224 | tf_op jit(solution)/shard_map/ppermute | solution.py:684
  231.4 15.9 %collective-permute-start.15 = (bf16[32,2048]{1,0:T(8,128)(2,1)}, bf16[32,2048]{1,0:T(8,128)(2,1)S(1)}, u32[]{:S(2)}, u32[]{:S(2)}) collective-permute-start(bf16[32,2048]{1,0:T(8,128)(2,1)} %get-tuple-element.125), channel_id=1, source_target_pairs={{0,24},{8,0},{16,8},{24,16},{1,25},{9,1},{17,9},{25,17},{2,26},{10... | collective-permute-start | bytes 393224 | tf_op jit(solution)/shard_map/ppermute | solution.py:684
  243.9 3.4 %copy-start.31 = (bf16[32,2048]{1,0:T(8,128)(2,1)}, bf16[32,2048]{1,0:T(8,128)(2,1)S(1)}, u32[]{:S(2)}) copy-start(bf16[32,2048]{1,0:T(8,128)(2,1)S(1)} %collective-permute-done.13.b_ref) | copy-start | bytes 393220
  247.3 0.7 copy-start.32
  247.3 0.7 copy-start.33
  247.3 1.1 copy-start.29
  250.7 19.0 %collective-permute-start.16 = (f32[40,1024]{1,0:T(8,128)}, f32[40,1024]{1,0:T(8,128)S(1)}, u32[]{:S(2)}, u32[]{:S(2)}) collective-permute-start(f32[40,1024]{1,0:T(8,128)} %get-tuple-element.131), channel_id=1, source_target_pairs={{0,0},{4,1},{8,2},{12,3},{16,4},{20,5},{24,6},{28,7},{32,8},{36,9}... | collective-permute-start | bytes 491528 | tf_op jit(solution)/shard_map/ppermute | solution.py:823
  252.3 15.2 %all-to-all-start.1 = ((bf16[4,8,1920]{2,1,0:T(8,128)(2,1)}), bf16[4,8,1920]{2,1,0:T(8,128)(2,1)S(1)}, u32[]{:S(2)}, u32[]{:S(2)}) async-start(bf16[4,8,1920]{2,1,0:T(8,128)(2,1)} %get-tuple-element.126), calls=%async_computation.4 | async-start | bytes 245760 | tf_op jit(solution)/shard_map/all_to_all | solution.py:822
  267.4 0.6 copy-start.30
  (1 other events, 0.6 us)
Sparse Core Ops, SparseCore 0:
  23.2 51.6 all-gather.1
  143.2 47.8 reduce-scatter.3
  193.6 29.2 reduce-scatter.7
  225.2 51.4 reduce-scatter.5
where the time goes:
time: 290 us; the launch traced here: 286 us
  Pallas kernels  140 us (48%)
  waiting for transfers between devices  59.9 us (21%)
  starting transfers between devices  42.3 us (15%)
  local copies, waits for them, and re-layouts  24.4 us (8%)
  between operations  14.6 us (5%)
  other arithmetic  5.12 us (2%)
    ppermute x15, waiting for transfers between devices, send(): lax.ppermute(value, axis, [(i, (i + step) % size) for i in range(size)])  49.3 us
    pallas_call x2, Pallas kernels, back(): pl.pallas_call(back_kernel, grid_spec=pltpu.PrefetchScalarGridSpec(num_sc...  37.4 us
    pallas_call x2, Pallas kernels, front(): pl.pallas_call(functools.partial(front_kernel, bool(known)), grid_spec=pl...  28.9 us
    pallas_call x2, Pallas kernels, attend(): pl.pallas_call(attend_kernel, grid_spec=pltpu.PrefetchScalarGridSpec(num_...  26.6 us
    ppermute x15, starting transfers between devices, send(): lax.ppermute(value, axis, [(i, (i + step) % size) for i in range(size)])  23.8 us
    unnamed x85, local copies, waits for them, and re-layouts  20.1 us
    pallas_call x1, Pallas kernels, grads_att(): pl.pallas_call(grads_att_kernel, grid_spec=pltpu.PrefetchScalarGridSpec(n...  10.6 us
    pallas_call x6, Pallas kernels, in_vmem(): pl.pallas_call(kernel, grid=(1,), in_specs=specs, out_specs=[whole(s[0])...  10.4 us
  transfers between devices with their start and end apart: 23, of which 9 were waited for; matrix products, arithmetic and copies ran while one was open for 3% of the time, Pallas kernels for 38%

commit v1 on v0

--- a/solution.py
+++ b/solution.py
@@ -505,15 +505,15 @@
 
 def finish(micro, x, cot, part, vectors, others, after=()):
     n, d = x.shape[2:]
-    tile = pl.BlockSpec((1, 1, 128, d), lambda i: (micro, 0, i, 0))
-    out = pl.BlockSpec((1, 128, d), lambda i: (micro, i, 0))
+    tile = pl.BlockSpec((1, 1, 256, d), lambda i: (micro, 0, i, 0))
+    out = pl.BlockSpec((1, 256, d), lambda i: (micro, i, 0))
     return pl.pallas_call(
         finish_kernel,
-        grid=(n // 128,),
+        grid=(n // 256,),
         in_specs=[tile] * 2
         + [
             pl.BlockSpec((8, d), lambda i: (0, 0)),
-            pl.BlockSpec((2, 128, d), lambda i: (0, i, 0)),
+            pl.BlockSpec((2, 256, d), lambda i: (0, i, 0)),
         ]
         + [ANY] * (len(others) + len(after)),
         out_specs=[out] * 2,
@@ -557,8 +557,8 @@
             at = 1024 + part * 256
             piece[:, at : at + 256] = qkv_ref[:, pl.ds(first, 256)]
         piece[:, 1792:1920] = block
-    rows_ref[0:32, :] = down_ref[...].astype(F32).astype(BF)
-    rows_ref[32:40, :] = out_ref[...].astype(F32).astype(BF)
+    rows = jnp.concatenate([down_ref[...].astype(F32), out_ref[...].astype(F32)], axis=0)
+    rows_ref[...] = rows.astype(BF)
 
 
 def to_payload_kernel(z_ref, g0_ref, g1_ref, g2_ref, g3_ref, rows_ref, after_ref, out_ref):

time: 290 us -> 290 us (level)
  no operation moved by 1% of the time
where the time goes in v1:
time: 290 us; the launch traced here: 287 us
  Pallas kernels  141 us (49%)
  waiting for transfers between devices  59.4 us (20%)
  starting transfers between devices  42.3 us (15%)
  local copies, waits for them, and re-layouts  24.4 us (8%)
  between operations  14.6 us (5%)
  other arithmetic  5.12 us (2%)
    ppermute x15, waiting for transfers between devices, send(): lax.ppermute(value, axis, [(i, (i + step) % size) for i in range(size)])  49.3 us
    pallas_call x2, Pallas kernels, back(): pl.pallas_call(back_kernel, grid_spec=pltpu.PrefetchScalarGridSpec(num_sc...  37.4 us
    pallas_call x2, Pallas kernels, front(): pl.pallas_call(functools.partial(front_kernel, bool(known)), grid_spec=pl...  28.9 us
    pallas_call x2, Pallas kernels, attend(): pl.pallas_call(attend_kernel, grid_spec=pltpu.PrefetchScalarGridSpec(num_...  26.6 us
    ppermute x15, starting transfers between devices, send(): lax.ppermute(value, axis, [(i, (i + step) % size) for i in range(size)])  23.8 us
    unnamed x85, local copies, waits for them, and re-layouts  20.1 us
    pallas_call x1, Pallas kernels, grads_att(): pl.pallas_call(grads_att_kernel, grid_spec=pltpu.PrefetchScalarGridSpec(n...  10.6 us
    pallas_call x6, Pallas kernels, in_vmem(): pl.pallas_call(kernel, grid=(1,), in_specs=specs, out_specs=[whole(s[0])...  10.4 us
  transfers between devices with their start and end apart: 23, of which 9 were waited for; matrix products, arithmetic and copies ran while one was open for 3% of the time, Pallas kernels for 38%

profile of v1, /device:TPU:0, one launch (start us, length us, event | category | flops | bytes accessed | tf_op | source)
XLA Modules:
  0.0 286.8 jit_solution(5943257092389414160)
XLA Ops:
  7.2 1.6 to_columns.1
  8.9 1.5 collective-permute-start.6
  10.4 2.5 collective-permute-start.3
  12.9 3.6 %collective-permute-start.4 = (bf16[8,1920]{1,0:T(8,128)(2,1)}, bf16[8,1920]{1,0:T(8,128)(2,1)S(1)}, u32[]{:S(2)}, u32[]{:S(2)}) collective-permute-start(bf16[8,1920]{1,0:T(8,128)(2,1)} %get-tuple-element.77), channel_id=1, source_target_pairs={{0,2},{1,3},{2,0},{3,1},{4,6},{5,7},{6,4},{7,5},{8,10},{9,11},{10,... | collective-permute-start | bytes 92168 | tf_op jit(solution)/shard_map/ppermute | solution.py:684
  16.5 1.7 collective-permute-start.5
  18.1 2.0 pack.2
  21.4 1.7 to_payload.1
  23.1 2.7 collective-permute-start.1
  25.9 1.1 collective-permute-start
  27.0 0.9 collective-permute-start.2
  29.1 21.8 %collective-permute-done.1.rest_2_.rest_0_ = bf16[512,1024]{1,0:T(8,128)(2,1)S(1)} collective-permute-done((bf16[512,1024]{1,0:T(8,128)(2,1)}, bf16[512,1024]{1,0:T(8,128)(2,1)S(1)}, u32[]{:S(2)}, u32[]{:S(2)}) %collective-permute-start.1) | collective-permute-done | bytes 1048608 | tf_op jit(solution)/shard_map/ppermute | solution.py:684
  51.0 1.1 copy-done.18
  52.0 2.1 pack.3
  54.1 3.7 %collective-permute-start.7 = (bf16[512,1024]{1,0:T(8,128)(2,1)}, bf16[512,1024]{1,0:T(8,128)(2,1)}, u32[]{:S(2)}, u32[]{:S(2)}) collective-permute-start(bf16[512,1024]{1,0:T(8,128)(2,1)} %bitcast.58), channel_id=1, source_target_pairs={{0,3},{1,0},{2,1},{3,2},{4,7},{5,4},{6,5},{7,6},{8,11},{9,8},{10,9... | collective-permute-start | bytes 3145736 | tf_op jit(solution)/shard_map/ppermute | solution.py:684
  57.8 0.9 collective-permute-start.9
  58.7 3.7 %fusion = (f32[2,1024,128]{2,1,0:T(8,128)S(1)}, f32[2,1024,128]{2,1,0:T(8,128)S(1)}) fusion(f32[128]{0:T(128)S(1)} %compare_select_fusion.3, f32[128]{0:T(128)S(1)} %compare_select_fusion.4, f32[2,1024]{1,0:T(2,128)S(1)} %fusion.2), kind=kLoop, calls=%fused_computation.3 | loop fusion | flops 524288 | bytes 2106368 | tf_op jit(solution)/shard_map/mul | solution.py:679
  62.4 1.4 fusion.10
  63.8 10.6 %collective-permute-done.rest_1_ = bf16[512,1024]{1,0:T(8,128)(2,1)S(1)} collective-permute-done((bf16[512,1024]{1,0:T(8,128)(2,1)}, bf16[512,1024]{1,0:T(8,128)(2,1)S(1)}, u32[]{:S(2)}, u32[]{:S(2)}) %collective-permute-start) | collective-permute-done | bytes 1048608 | tf_op jit(solution)/shard_map/ppermute | solution.py:684
  74.4 1.0 copy-done.22
  75.4 1.0 copy-done.24
  76.4 1.0 copy-done.13
  77.5 1.0 copy-done.14
  78.5 1.2 copy-done.19
  79.7 1.2 copy-done.23
  81.0 1.2 copy-done.25
  82.2 13.8 %front.2 = (bf16[1,1024,1024]{2,1,0:T(8,128)(2,1)S(1)}, bf16[1,1024,1024]{2,1,0:T(8,128)(2,1)S(1)}, bf16[1,1024,1024]{2,1,0:T(8,128)(2,1)S(1)}, bf16[1,1024,1024...) custom-call(s32[1]{0:T(128)} %bitcast.z_ref, ...), custom_call_target="tpu_custom_call" | custom-call | flops 1024 | bytes 1024 | tf_op jit(solution)/shard_map/front/pallas_call | solution.py:200
  96.1 1.4 copy-done.21
  97.4 13.3 %attend.2 = (bf16[1,1024,256]{2,1,0:T(8,128)(2,1)S(1)}, bf16[1,3,1024,256]{3,2,1,0:T(8,128)(2,1)S(1)}, f32[3,8,256]{2,1,0:T(8,128)S(1)}) custom-call(s32[1]{0:T(128)} %bitcast.z_ref, bf16[1,1024,256]{2,1,0:T(8,128)(2,1)S(1)} %get-tuple-element.83.q_ref, bf16[1,1024,256]{2,1,0:T(8,128)(2,1)S(1)} %get-tuple-element.84.k_ref, ...), custom_call_target="tpu_custom_call" | custom-call | flops 1024 | bytes 1024 | tf_op jit(solution)/shard_map/attend/pallas_call | solution.py:312
  110.8 5.7 %grads_mlp0.1.rest_0_.sum_ref = bf16[1024,2048]{1,0:T(8,128)(2,1)S(1)} custom-call(bf16[1,1024,1024]{2,1,0:T(8,128)(2,1)S(1)} %get-tuple-element.92.n_ref.n0_ref, bf16[1,1024,1024]{2,1,0:T(8,128)(2,1)S(1)} %get-tuple-element.88.dup_ref, bf16[1,1024,1024]{2,1,0:T(8,128)(2,1)S(1)} %get-tuple-element.82.act_ref, ...), custom_call_target="tpu_custom_call" | custom-call | flops 1024 | bytes 1024 | tf_op jit(solution)/shard_map/grads_mlp0/pallas_call | solution.py:417
  116.5 2.0 copy-done
  118.6 24.4 %back.2 = (bf16[2048,1024]{1,0:T(8,128)(2,1)}, f32[8,1024]{1,0:T(8,128)S(1)}, f32[8,1024]{1,0:T(8,128)S(1)}) custom-call(s32[1]{0:T(128)} %bitcast.z_ref, bf16[1,1024,1024]{2,1,0:T(8,128)(2,1)} %copy-done.2, bf16[1,1024,256]{2,1,0:T(8,128)(2,1)S(1)} %get-tuple-element.87.rest_0_.mix_ref.mix0_ref, bf16[1,1024,1024]{2,1,0:T(8,128)(2,1)} %copy-done.3, ...), custom_call_target="tpu_custom_call" | custom-call | flops 1024 | bytes 1024 | tf_op jit(solution)/shard_map/back/pallas_call | solution.py:368
  143.2 0.9 copy-done.10
  144.8 15.1 %front.3 = (bf16[1,1024,1024]{2,1,0:T(8,128)(2,1)}, bf16[1,1024,1024]{2,1,0:T(8,128)(2,1)}, bf16[1,1024,1024]{2,1,0:T(8,128)(2,1)}, bf16[1,1024,1024]{2,1,0:T(8,...) custom-call(s32[1]{0:T(128)} %bitcast.z_ref, ...), custom_call_target="tpu_custom_call" | custom-call | flops 1024 | bytes 1024 | tf_op jit(solution)/shard_map/front/pallas_call | solution.py:200
  159.8 1.8 copy-done.6
  161.7 8.5 %grads_mlp1.1 = (bf16[512,2048]{1,0:T(8,128)(2,1)S(1)}, bf16[512,2048]{1,0:T(8,128)(2,1)S(1)}) custom-call(s32[1]{0:T(128)} %bitcast.8.c_ref, bf16[1,1024,1024]{2,1,0:T(8,128)(2,1)S(1)} %copy-done.6, bf16[1,1024,1024]{2,1,0:T(8,128)(2,1)} %get-tuple-element.101.dup_ref, bf16[1,1024,1024]{2,1,0:T(8,128)(2,1)} %get-tuple-element.95.act_ref, ...), custom_call_target="tpu_custom_call" | custom-call | flops 1024 | bytes 1024 | tf_op jit(solution)/shard_map/grads_mlp1/pallas_call | solution.py:433
  170.3 13.3 %attend.3 = (bf16[1,1024,256]{2,1,0:T(8,128)(2,1)S(1)}, bf16[1,3,1024,256]{3,2,1,0:T(8,128)(2,1)S(1)}, f32[3,8,256]{2,1,0:T(8,128)S(1)}) custom-call(s32[1]{0:T(128)} %bitcast.z_ref, bf16[1,1024,256]{2,1,0:T(8,128)(2,1)S(1)} %get-tuple-element.96.q_ref, bf16[1,1024,256]{2,1,0:T(8,128)(2,1)S(1)} %get-tuple-element.97.k_ref, ...), custom_call_target="tpu_custom_call" | custom-call | flops 1024 | bytes 1024 | tf_op jit(solution)/shard_map/attend/pallas_call | solution.py:312
  183.6 1.1 copy-done.8
  184.7 2.1 add_after.1.rest_0_
  186.9 10.6 %grads_att.1 = (bf16[512,1024]{1,0:T(8,128)(2,1)}, bf16[512,1024]{1,0:T(8,128)(2,1)}) custom-call(s32[1]{0:T(128)} %bitcast.8.c_ref, bf16[1,1024,1024]{2,1,0:T(8,128)(2,1)} %copy-done.5, bf16[1,1024,1024]{2,1,0:T(8,128)(2,1)} %get-tuple-element.100.n_ref.n1_ref, bf16[1,3,1024,256]{3,2,1,0:T(8,128)(2,1)} %copy-done.7, bf16[1,3,1024,256]{3,2,1,0:T(8,128)(2,1)} %copy-done.8, ...), custom_call_target="tpu_custom_call" | custom-call | flops 1024 | bytes 1024 | tf_op jit(solution)/shard_map/grads_att/pallas_call | solution.py:474
  197.5 12.9 %back.3 = (bf16[2048,1024]{1,0:T(8,128)(2,1)}, f32[8,1024]{1,0:T(8,128)}, f32[8,1024]{1,0:T(8,128)}) custom-call(s32[1]{0:T(128)} %bitcast.z_ref, bf16[1,1024,1024]{2,1,0:T(8,128)(2,1)} %get-tuple-element.95.act_ref, bf16[1,1024,256]{2,1,0:T(8,128)(2,1)} %copy-done.12, bf16[1,1024,1024]{2,1,0:T(8,128)(2,1)} %get-tuple-element.101.dup_ref, ...), custom_call_target="tpu_custom_call" | custom-call | flops 1024 | bytes 1024 | tf_op jit(solution)/shard_map/back/pallas_call | solution.py:368
  210.7 1.0 copy-done.28
  213.3 0.7 stack.28
  214.2 1.1 collective-permute-done.11.got_ref
  215.3 0.8 collective-permute-done.12.vb_ref
  216.0 1.3 to_xy.1
  217.3 7.6 %all-to-all-start = ((bf16[16,32,1152]{2,1,0:T(8,128)(2,1)}), bf16[16,32,1152]{2,1,0:T(8,128)(2,1)S(1)}, u32[]{:S(2)}, u32[]{:S(2)}) async-start(bf16[16,32,1152]{2,1,0:T(8,128)(2,1)} %to_xy.1), calls=%async_computation.2 | async-start | bytes 2359296 | tf_op jit(solution)/shard_map/all_to_all | solution.py:815
  225.0 1.8 to_y.1
  226.8 1.9 collective-permute-start.13
  228.7 2.7 collective-permute-start.14
  231.4 1.5 collective-permute-start.15
  232.9 11.0 %collective-permute-done.13.b_ref = bf16[32,2048]{1,0:T(8,128)(2,1)S(1)} collective-permute-done((bf16[32,2048]{1,0:T(8,128)(2,1)}, bf16[32,2048]{1,0:T(8,128)(2,1)S(1)}, u32[]{:S(2)}, u32[]{:S(2)}) %collective-permute-start.13) | collective-permute-done | bytes 131104 | tf_op jit(solution)/shard_map/ppermute | solution.py:684
  243.9 3.4 %collective-permute-done.14.c_ref = bf16[32,2048]{1,0:T(8,128)(2,1)S(1)} collective-permute-done((bf16[32,2048]{1,0:T(8,128)(2,1)}, bf16[32,2048]{1,0:T(8,128)(2,1)S(1)}, u32[]{:S(2)}, u32[]{:S(2)}) %collective-permute-start.14) | collective-permute-done | bytes 131104 | tf_op jit(solution)/shard_map/ppermute | solution.py:684
  247.3 0.6 copy-done.32
  248.4 2.3 to_z.1
  250.7 1.6 collective-permute-start.16
  252.3 7.6 %all-to-all-start.1 = ((bf16[4,8,1920]{2,1,0:T(8,128)(2,1)}), bf16[4,8,1920]{2,1,0:T(8,128)(2,1)S(1)}, u32[]{:S(2)}, u32[]{:S(2)}) async-start(bf16[4,8,1920]{2,1,0:T(8,128)(2,1)} %get-tuple-element.126), calls=%async_computation.4 | async-start | bytes 245760 | tf_op jit(solution)/shard_map/all_to_all | solution.py:822
  259.8 3.3 %finish.2 = (bf16[2,256,1024]{2,1,0:T(8,128)(2,1)}, f32[2,256,1024]{2,1,0:T(8,128)}) custom-call(bf16[2,1,256,1024]{3,2,1,0:T(8,128)(2,1)} %x_ref.3, bf16[2,1,256,1024]{3,2,1,0:T(8,128)(2,1)} %c_ref.3, f32[8,1024]{1,0:T(8,128)} %copy-done.27, bf16[2,256,1024]{2,1,0:T(8,128)(2,1)} %bitcast.64), custom_call_target="tpu_custom_call" | custom-call | flops 1024 | bytes 1024 | tf_op jit(solution)/shard_map/finish/pallas_call | solution.py:510
  263.2 4.3 %all-to-all-done.1.home_ref = bf16[4,8,1920]{2,1,0:T(8,128)(2,1)S(1)} async-done(((bf16[4,8,1920]{2,1,0:T(8,128)(2,1)}), bf16[4,8,1920]{2,1,0:T(8,128)(2,1)S(1)}, u32[]{:S(2)}, u32[]{:S(2)}) %all-to-all-start.1) | async-done | bytes 122912 | tf_op jit(solution)/shard_map/all_to_all | solution.py:822
  267.4 0.6 copy-done.30
  268.1 1.6 home.1
  269.7 0.7 slice.88
  270.4 0.6 slice.87
  271.0 5.7 %reduce-scatter.6.cloned.1.call-done = bf16[512,1024]{1,0:T(8,128)(2,1)} async-done(((bf16[2048,1024]{1,0:T(8,128)(2,1)}), bf16[512,1024]{1,0:T(8,128)(2,1)}) %reduce-scatter.6.cloned.1.call-update) | async-done | bytes 1048592 | tf_op jit(solution)/shard_map/reduce_scatter | solution.py:778
  276.7 3.3 %finish.3 = (bf16[2,256,1024]{2,1,0:T(8,128)(2,1)}, f32[2,256,1024]{2,1,0:T(8,128)}) custom-call(bf16[2,1,256,1024]{3,2,1,0:T(8,128)(2,1)} %x_ref.3, bf16[2,1,256,1024]{3,2,1,0:T(8,128)(2,1)} %c_ref.3, f32[8,1024]{1,0:T(8,128)} %copy-done.27, bf16[2,256,1024]{2,1,0:T(8,128)(2,1)} %bitcast.66, ...), custom_call_target="tpu_custom_call", output_to_operand_aliasing={{0}: (4, {}), {1}: (5, {})} | custom-call | flops 1024 | bytes 1024 | tf_op jit(solution)/shard_map/finish/pallas_call | solution.py:510
  (135 shorter events, 5.7 us)
Async XLA Ops:
  7.2 69.2 %all-gather.2.cloned.1.call-start = ((), (), s32[]{:S(2)}) async-start(), calls=%async_computation.5 | async-start | bytes 6758400 | tf_op jit(solution)/shard_map/all_gather | solution.py:737
  8.9 11.8 %collective-permute-start.6 = (bf16[40,1024]{1,0:T(8,128)(2,1)}, bf16[40,1024]{1,0:T(8,128)(2,1)S(1)}, u32[]{:S(2)}, u32[]{:S(2)}) collective-permute-start(bf16[40,1024]{1,0:T(8,128)(2,1)} %get-tuple-element.79), channel_id=1, source_target_pairs={{0,0},{1,4},{2,8},{3,12},{4,16},{5,20},{6,24},{7,28},{8,32},{9,36}... | collective-permute-start | bytes 245768 | tf_op jit(solution)/shard_map/ppermute | solution.py:727
  10.4 9.7 %collective-permute-start.3 = (bf16[8,1920]{1,0:T(8,128)(2,1)}, bf16[8,1920]{1,0:T(8,128)(2,1)S(1)}, u32[]{:S(2)}, u32[]{:S(2)}) collective-permute-start(bf16[8,1920]{1,0:T(8,128)(2,1)} %get-tuple-element.76), channel_id=1, source_target_pairs={{0,1},{1,2},{2,3},{3,0},{4,5},{5,6},{6,7},{7,4},{8,9},{9,10},{10,1... | collective-permute-start | bytes 92168 | tf_op jit(solution)/shard_map/ppermute | solution.py:684
  12.9 7.3 %collective-permute-start.4 = (bf16[8,1920]{1,0:T(8,128)(2,1)}, bf16[8,1920]{1,0:T(8,128)(2,1)S(1)}, u32[]{:S(2)}, u32[]{:S(2)}) collective-permute-start(bf16[8,1920]{1,0:T(8,128)(2,1)} %get-tuple-element.77), channel_id=1, source_target_pairs={{0,2},{1,3},{2,0},{3,1},{4,6},{5,7},{6,4},{7,5},{8,10},{9,11},{10,... | collective-permute-start | bytes 92168 | tf_op jit(solution)/shard_map/ppermute | solution.py:684
  16.4 11.5 %copy-start.35 = (s32[2,1,1024]{2,1,0:T(1,128)S(1)}, s32[2,1,1024]{2,1,0:T(1,128)}, u32[]{:S(2)}) copy-start(s32[2,1,1024]{2,1,0:T(1,128)} %param.15) | copy-start | bytes 24580
  16.5 4.3 %collective-permute-start.5 = (bf16[8,1920]{1,0:T(8,128)(2,1)}, bf16[8,1920]{1,0:T(8,128)(2,1)S(1)}, u32[]{:S(2)}, u32[]{:S(2)}) collective-permute-start(bf16[8,1920]{1,0:T(8,128)(2,1)} %get-tuple-element.78), channel_id=1, source_target_pairs={{0,3},{1,0},{2,1},{3,2},{4,7},{5,4},{6,5},{7,6},{8,11},{9,8},{10,9... | collective-permute-start | bytes 92168 | tf_op jit(solution)/shard_map/ppermute | solution.py:684
  20.1 0.6 copy-start.38
  20.2 0.6 copy-start.39
  20.7 0.6 copy-start.34
  23.1 174.5 %reduce-scatter.4.cloned.1.call-start = ((), (), s32[]{:S(2)}) async-start(), calls=%async_computation.6 | async-start | bytes 5242880 | tf_op jit(solution)/shard_map/reduce_scatter | solution.py:765
  23.1 27.8 %collective-permute-start.1 = (bf16[512,1024]{1,0:T(8,128)(2,1)}, bf16[512,1024]{1,0:T(8,128)(2,1)S(1)}, u32[]{:S(2)}, u32[]{:S(2)}) collective-permute-start(bf16[512,1024]{1,0:T(8,128)(2,1)} %bitcast.54), channel_id=1, source_target_pairs={{0,2},{1,3},{2,0},{3,1},{4,6},{5,7},{6,4},{7,5},{8,10},{9,11},{10,... | collective-permute-start | bytes 3145736 | tf_op jit(solution)/shard_map/ppermute | solution.py:684
  25.9 48.6 %collective-permute-start = (bf16[512,1024]{1,0:T(8,128)(2,1)}, bf16[512,1024]{1,0:T(8,128)(2,1)S(1)}, u32[]{:S(2)}, u32[]{:S(2)}) collective-permute-start(bf16[512,1024]{1,0:T(8,128)(2,1)} %bitcast.55), channel_id=1, source_target_pairs={{0,3},{1,0},{2,1},{3,2},{4,7},{5,4},{6,5},{7,6},{8,11},{9,8},{10,9... | collective-permute-start | bytes 3145736 | tf_op jit(solution)/shard_map/ppermute | solution.py:684
  27.0 48.5 %collective-permute-start.2 = (bf16[512,1024]{1,0:T(8,128)(2,1)}, bf16[512,1024]{1,0:T(8,128)(2,1)S(1)}, u32[]{:S(2)}, u32[]{:S(2)}) collective-permute-start(bf16[512,1024]{1,0:T(8,128)(2,1)} %bitcast.56), channel_id=1, source_target_pairs={{0,1},{1,2},{2,3},{3,0},{4,5},{5,6},{6,7},{7,4},{8,9},{9,10},{10,1... | collective-permute-start | bytes 3145736 | tf_op jit(solution)/shard_map/ppermute | solution.py:684
  29.1 29.5 %copy-start.41 = (s32[2,1,1024]{2,1,0:T(1,128)S(1)}, s32[2,1,1024]{2,1,0:T(1,128)}, u32[]{:S(2)}) copy-start(s32[2,1,1024]{2,1,0:T(1,128)} %param.16) | copy-start | bytes 24580
  51.0 1.1 copy-start.18
  54.1 64.5 %collective-permute-start.7 = (bf16[512,1024]{1,0:T(8,128)(2,1)}, bf16[512,1024]{1,0:T(8,128)(2,1)}, u32[]{:S(2)}, u32[]{:S(2)}) collective-permute-start(bf16[512,1024]{1,0:T(8,128)(2,1)} %bitcast.58), channel_id=1, source_target_pairs={{0,3},{1,0},{2,1},{3,2},{4,7},{5,4},{6,5},{7,6},{8,11},{9,8},{10,9... | collective-permute-start | bytes 3145736 | tf_op jit(solution)/shard_map/ppermute | solution.py:684
  57.8 60.8 %collective-permute-start.8 = (bf16[512,1024]{1,0:T(8,128)(2,1)}, bf16[512,1024]{1,0:T(8,128)(2,1)}, u32[]{:S(2)}, u32[]{:S(2)}) collective-permute-start(bf16[512,1024]{1,0:T(8,128)(2,1)} %bitcast.59), channel_id=1, source_target_pairs={{0,2},{1,3},{2,0},{3,1},{4,6},{5,7},{6,4},{7,5},{8,10},{9,11},{10,... | collective-permute-start | bytes 3145736 | tf_op jit(solution)/shard_map/ppermute | solution.py:684
  57.8 60.8 %collective-permute-start.9 = (bf16[512,1024]{1,0:T(8,128)(2,1)}, bf16[512,1024]{1,0:T(8,128)(2,1)}, u32[]{:S(2)}, u32[]{:S(2)}) collective-permute-start(bf16[512,1024]{1,0:T(8,128)(2,1)} %bitcast.60), channel_id=1, source_target_pairs={{0,1},{1,2},{2,3},{3,0},{4,5},{5,6},{6,7},{7,4},{8,9},{9,10},{10,1... | collective-permute-start | bytes 3145736 | tf_op jit(solution)/shard_map/ppermute | solution.py:684
  62.4 14.0 %copy-start.1 = (bf16[2,256,1024]{2,1,0:T(8,128)(2,1)S(1)}, bf16[2,256,1024]{2,1,0:T(8,128)(2,1)}, u32[]{:S(2)}) copy-start(bf16[2,256,1024]{2,1,0:T(8,128)(2,1)} %pack.2) | copy-start | bytes 3145732
  74.4 1.0 copy-start.22
  75.4 1.0 copy-start.24
  76.4 1.0 copy-start.13
  77.5 1.0 copy-start.14
  78.5 1.2 copy-start.19
  79.7 1.2 copy-start.23
  81.0 1.2 copy-start.25
  96.0 1.4 copy-start.21
  97.4 19.1 %copy-start.2 = (bf16[1,1024,1024]{2,1,0:T(8,128)(2,1)}, bf16[1,1024,1024]{2,1,0:T(8,128)(2,1)S(1)}, u32[]{:S(2)}) copy-start(bf16[1,1024,1024]{2,1,0:T(8,128)(2,1)S(1)} %get-tuple-element.82.act_ref) | copy-start | bytes 6291460
  97.4 19.1 %copy-start.3 = (bf16[1,1024,1024]{2,1,0:T(8,128)(2,1)}, bf16[1,1024,1024]{2,1,0:T(8,128)(2,1)S(1)}, u32[]{:S(2)}) copy-start(bf16[1,1024,1024]{2,1,0:T(8,128)(2,1)S(1)} %get-tuple-element.88.dup_ref) | copy-start | bytes 6291460
  97.4 19.1 %copy-start.4 = (bf16[1,1024,1024]{2,1,0:T(8,128)(2,1)}, bf16[1,1024,1024]{2,1,0:T(8,128)(2,1)S(1)}, u32[]{:S(2)}) copy-start(bf16[1,1024,1024]{2,1,0:T(8,128)(2,1)S(1)} %get-tuple-element.93.cot_ref.cot0_ref) | copy-start | bytes 6291460
  97.4 19.1 %copy-start.5 = (bf16[1,1024,1024]{2,1,0:T(8,128)(2,1)}, bf16[1,1024,1024]{2,1,0:T(8,128)(2,1)S(1)}, u32[]{:S(2)}) copy-start(bf16[1,1024,1024]{2,1,0:T(8,128)(2,1)S(1)} %get-tuple-element.92.n_ref.n0_ref) | copy-start | bytes 6291460
  97.4 21.2 %copy-start.9 = (bf16[256,1024]{1,0:T(8,128)(2,1)}, bf16[256,1024]{1,0:T(8,128)(2,1)S(1)}, u32[]{:S(2)}) copy-start(bf16[256,1024]{1,0:T(8,128)(2,1)S(1)} %get-tuple-element.81.wo_ref.rest_5_) | copy-start | bytes 1572868
  97.4 45.7 %copy-start.27 = (f32[8,1024]{1,0:T(8,128)}, f32[8,1024]{1,0:T(8,128)S(1)}, u32[]{:S(2)}) copy-start(f32[8,1024]{1,0:T(8,128)S(1)} %get-tuple-element.80.rest_6_.vec_ref) | copy-start | bytes 98308
  110.7 7.9 %copy-start.7 = (bf16[1,3,1024,256]{3,2,1,0:T(8,128)(2,1)}, bf16[1,3,1024,256]{3,2,1,0:T(8,128)(2,1)S(1)}, u32[]{:S(2)}) copy-start(bf16[1,3,1024,256]{3,2,1,0:T(8,128)(2,1)S(1)} %get-tuple-element.89.dqkv_ref.dqkv0_ref) | copy-start | bytes 4718596
  110.7 7.9 %copy-start.11 = (bf16[1,1024,256]{2,1,0:T(8,128)(2,1)}, bf16[1,1024,256]{2,1,0:T(8,128)(2,1)S(1)}, u32[]{:S(2)}) copy-start(bf16[1,1024,256]{2,1,0:T(8,128)(2,1)S(1)} %get-tuple-element.87.rest_0_.mix_ref.mix0_ref) | copy-start | bytes 1572868
  116.5 2.0 copy-start
  143.0 1.0 copy-start.10
  143.1 1.2 copy-start.15
  143.1 1.4 copy-start.16
  143.1 1.7 copy-start.17
  143.1 81.9 %reduce-scatter.8.cloned.1.call-start = ((), (), s32[]{:S(2)}) async-start(), calls=%async_computation.8 | async-start | bytes 2621440 | tf_op jit(solution)/shard_map/reduce_scatter | solution.py:774
  159.8 10.3 %copy-start.26 = (f32[1,1024,128]{2,1,0:T(8,128)}, f32[1,1024,128]{2,1,0:T(8,128)S(1)}, u32[]{:S(2)}) copy-start(f32[1,1024,128]{2,1,0:T(8,128)S(1)} %get-tuple-element.107.stat_ref) | copy-start | bytes 1572868
  159.8 1.8 copy-start.6
  170.2 14.5 %collective-permute-start.10 = (bf16[512,2048]{1,0:T(8,128)(2,1)S(1)}, bf16[512,2048]{1,0:T(8,128)(2,1)S(1)}, u32[]{:S(2)}, u32[]{:S(2)}) collective-permute-start(bf16[512,2048]{1,0:T(8,128)(2,1)S(1)} %get-tuple-element.108), channel_id=1, source_target_pairs={{0,4},{4,0},{1,5},{5,1},{2,6},{6,2},{3,7},{7,3},{8,12},{12,8},{9,1... | collective-permute-start | bytes 6291464 | tf_op jit(solution)/shard_map/ppermute | solution.py:684
  183.5 1.1 copy-start.8
  184.7 2.1 copy-start.12
  186.9 89.8 %reduce-scatter.6.cloned.1.call-start = ((), (), s32[]{:S(2)}) async-start(), calls=%async_computation.7 | async-start | bytes 5242880 | tf_op jit(solution)/shard_map/reduce_scatter | solution.py:778
  210.5 1.2 copy-start.28
  210.5 2.5 copy-start.37
  210.5 2.6 copy-start.36
  210.5 5.5 %copy-start.20 = (bf16[512,1024]{1,0:T(8,128)(2,1)S(1)}, bf16[512,1024]{1,0:T(8,128)(2,1)}, u32[]{:S(2)}) copy-start(bf16[512,1024]{1,0:T(8,128)(2,1)} %get-tuple-element.109.rest_1_.own_ref) | copy-start | bytes 3145732
  212.2 3.1 %collective-permute-start.11 = (bf16[512,1024]{1,0:T(8,128)(2,1)}, bf16[512,1024]{1,0:T(8,128)(2,1)S(1)}, u32[]{:S(2)}, u32[]{:S(2)}) collective-permute-start(bf16[512,1024]{1,0:T(8,128)(2,1)} %get-tuple-element.113), channel_id=1, source_target_pairs={{0,4},{4,0},{1,5},{5,1},{2,6},{6,2},{3,7},{7,3},{8,12},{12,8},{9,1... | collective-permute-start | bytes 3145736 | tf_op jit(solution)/shard_map/ppermute | solution.py:684
  214.0 2.0 collective-permute-start.12
  217.3 30.0 %all-to-all-start = ((bf16[16,32,1152]{2,1,0:T(8,128)(2,1)}), bf16[16,32,1152]{2,1,0:T(8,128)(2,1)S(1)}, u32[]{:S(2)}, u32[]{:S(2)}) async-start(bf16[16,32,1152]{2,1,0:T(8,128)(2,1)} %to_xy.1), calls=%async_computation.2 | async-start | bytes 2359296 | tf_op jit(solution)/shard_map/all_to_all | solution.py:815
  226.8 17.1 %collective-permute-start.13 = (bf16[32,2048]{1,0:T(8,128)(2,1)}, bf16[32,2048]{1,0:T(8,128)(2,1)S(1)}, u32[]{:S(2)}, u32[]{:S(2)}) collective-permute-start(bf16[32,2048]{1,0:T(8,128)(2,1)} %get-tuple-element.123), channel_id=1, source_target_pairs={{0,8},{8,16},{16,24},{24,0},{1,9},{9,17},{17,25},{25,1},{2,10},{10... | collective-permute-start | bytes 393224 | tf_op jit(solution)/shard_map/ppermute | solution.py:684
  228.7 18.5 %collective-permute-start.14 = (bf16[32,2048]{1,0:T(8,128)(2,1)}, bf16[32,2048]{1,0:T(8,128)(2,1)S(1)}, u32[]{:S(2)}, u32[]{:S(2)}) collective-permute-start(bf16[32,2048]{1,0:T(8,128)(2,1)} %get-tuple-element.124), channel_id=1, source_target_pairs={{0,16},{8,24},{16,0},{24,8},{1,17},{9,25},{17,1},{25,9},{2,18},{10... | collective-permute-start | bytes 393224 | tf_op jit(solution)/shard_map/ppermute | solution.py:684
  231.4 15.9 %collective-permute-start.15 = (bf16[32,2048]{1,0:T(8,128)(2,1)}, bf16[32,2048]{1,0:T(8,128)(2,1)S(1)}, u32[]{:S(2)}, u32[]{:S(2)}) collective-permute-start(bf16[32,2048]{1,0:T(8,128)(2,1)} %get-tuple-element.125), channel_id=1, source_target_pairs={{0,24},{8,0},{16,8},{24,16},{1,25},{9,1},{17,9},{25,17},{2,26},{10... | collective-permute-start | bytes 393224 | tf_op jit(solution)/shard_map/ppermute | solution.py:684
  243.9 3.4 %copy-start.31 = (bf16[32,2048]{1,0:T(8,128)(2,1)}, bf16[32,2048]{1,0:T(8,128)(2,1)S(1)}, u32[]{:S(2)}) copy-start(bf16[32,2048]{1,0:T(8,128)(2,1)S(1)} %collective-permute-done.13.b_ref) | copy-start | bytes 393220
  247.3 0.7 copy-start.32
  247.3 0.7 copy-start.33
  247.3 1.1 copy-start.29
  250.7 19.0 %collective-permute-start.16 = (f32[40,1024]{1,0:T(8,128)}, f32[40,1024]{1,0:T(8,128)S(1)}, u32[]{:S(2)}, u32[]{:S(2)}) collective-permute-start(f32[40,1024]{1,0:T(8,128)} %get-tuple-element.131), channel_id=1, source_target_pairs={{0,0},{4,1},{8,2},{12,3},{16,4},{20,5},{24,6},{28,7},{32,8},{36,9}... | collective-permute-start | bytes 491528 | tf_op jit(solution)/shard_map/ppermute | solution.py:823
  252.3 15.2 %all-to-all-start.1 = ((bf16[4,8,1920]{2,1,0:T(8,128)(2,1)}), bf16[4,8,1920]{2,1,0:T(8,128)(2,1)S(1)}, u32[]{:S(2)}, u32[]{:S(2)}) async-start(bf16[4,8,1920]{2,1,0:T(8,128)(2,1)} %get-tuple-element.126), calls=%async_computation.4 | async-start | bytes 245760 | tf_op jit(solution)/shard_map/all_to_all | solution.py:822
  267.4 0.6 copy-start.30
  (1 other events, 0.6 us)
Sparse Core Ops, SparseCore 0:
  23.2 51.6 all-gather.1
  143.2 47.8 reduce-scatter.3
  193.6 29.2 reduce-scatter.7
  225.2 51.4 reduce-scatter.5

commit v2 on v0

--- a/solution.py
+++ b/solution.py
@@ -557,8 +557,8 @@
             at = 1024 + part * 256
             piece[:, at : at + 256] = qkv_ref[:, pl.ds(first, 256)]
         piece[:, 1792:1920] = block
-    rows_ref[0:32, :] = down_ref[...].astype(F32).astype(BF)
-    rows_ref[32:40, :] = out_ref[...].astype(F32).astype(BF)
+    rows = jnp.concatenate([down_ref[...].astype(F32), out_ref[...].astype(F32)], axis=0)
+    rows_ref[...] = rows.astype(BF)
 
 
 def to_payload_kernel(z_ref, g0_ref, g1_ref, g2_ref, g3_ref, rows_ref, after_ref, out_ref):
@@ -760,7 +760,7 @@
     mix0, dqkv0, bqkv0 = run_attend(0, heads0, (), 30)
     first = grads_mlp0(n0, dup0, act0, cot0, (mix0,))
     cuts0, gain0, shift0 = back(
-        z_arr, act0, mix0, dup0, dqkv0, hid0, stat0, weights, w_o, (first, *pieces1[1:]), 46
+        z_arr, act0, mix0, dup0, dqkv0, hid0, stat0, weights, w_o, (first, *pieces1[1:]), 24
     )
     sum0 = lax.psum_scatter(cuts0, "z", scatter_dimension=0, tiled=True)
     hid1, cot1, n1, act1, dup1, *heads1, stat1, bup1 = front(

time: 290 us -> 289 us (level)
  waiting for transfers between devices: 59.9 us -> 63.2 us
    unnamed x85 -> x87, local copies, waits for them, and re-layouts: 20.1 us -> 18.7 us
  transfers between devices with their start and end apart: 23 -> 23, of which waited for: 9 -> 10; matrix products, arithmetic and copies ran while one was open for 3% -> 3% of each run, Pallas kernels for 38% -> 38%
where the time goes in v2:
time: 289 us; the launch traced here: 286 us
  Pallas kernels  138 us (48%)
  waiting for transfers between devices  63.2 us (22%)
  starting transfers between devices  42.5 us (15%)
  local copies, waits for them, and re-layouts  23 us (8%)
  between operations  14.6 us (5%)
  other arithmetic  5.12 us (2%)
    ppermute x15, waiting for transfers between devices, send(): lax.ppermute(value, axis, [(i, (i + step) % size) for i in range(size)])  51.8 us
    pallas_call x2, Pallas kernels, back(): pl.pallas_call(back_kernel, grid_spec=pltpu.PrefetchScalarGridSpec(num_sc...  35.1 us
    pallas_call x2, Pallas kernels, front(): pl.pallas_call(functools.partial(front_kernel, bool(known)), grid_spec=pl...  28.9 us
    pallas_call x2, Pallas kernels, attend(): pl.pallas_call(attend_kernel, grid_spec=pltpu.PrefetchScalarGridSpec(num_...  26.6 us
    ppermute x15, starting transfers between devices, send(): lax.ppermute(value, axis, [(i, (i + step) % size) for i in range(size)])  23.9 us
    unnamed x87, local copies, waits for them, and re-layouts  18.7 us
    pallas_call x1, Pallas kernels, grads_att(): pl.pallas_call(grads_att_kernel, grid_spec=pltpu.PrefetchScalarGridSpec(n...  10.6 us
    pallas_call x6, Pallas kernels, in_vmem(): pl.pallas_call(kernel, grid=(1,), in_specs=specs, out_specs=[whole(s[0])...  10.4 us
  transfers between devices with their start and end apart: 23, of which 10 were waited for; matrix products, arithmetic and copies ran while one was open for 3% of the time, Pallas kernels for 38%

profile of v2, /device:TPU:0, one launch (start us, length us, event | category | flops | bytes accessed | tf_op | source)
XLA Modules:
  0.0 286.2 jit_solution(7643882538277515054)
XLA Ops:
  7.2 1.6 to_columns.1
  8.9 1.5 collective-permute-start.6
  10.4 2.5 collective-permute-start.3
  12.9 3.6 %collective-permute-start.4 = (bf16[8,1920]{1,0:T(8,128)(2,1)}, bf16[8,1920]{1,0:T(8,128)(2,1)S(1)}, u32[]{:S(2)}, u32[]{:S(2)}) collective-permute-start(bf16[8,1920]{1,0:T(8,128)(2,1)} %get-tuple-element.77), channel_id=1, source_target_pairs={{0,2},{1,3},{2,0},{3,1},{4,6},{5,7},{6,4},{7,5},{8,10},{9,11},{10,... | collective-permute-start | bytes 92168 | tf_op jit(solution)/shard_map/ppermute | solution.py:684
  16.5 1.7 collective-permute-start.5
  18.1 2.0 pack.2
  21.4 1.7 to_payload.1
  23.1 2.7 collective-permute-start.1
  25.9 1.1 collective-permute-start
  27.0 0.9 collective-permute-start.2
  29.1 21.8 %collective-permute-done.1.rest_2_.rest_0_ = bf16[512,1024]{1,0:T(8,128)(2,1)S(1)} collective-permute-done((bf16[512,1024]{1,0:T(8,128)(2,1)}, bf16[512,1024]{1,0:T(8,128)(2,1)S(1)}, u32[]{:S(2)}, u32[]{:S(2)}) %collective-permute-start.1) | collective-permute-done | bytes 1048608 | tf_op jit(solution)/shard_map/ppermute | solution.py:684
  51.0 1.0 copy-done.18
  51.9 2.1 pack.3
  54.0 3.7 %collective-permute-start.7 = (bf16[512,1024]{1,0:T(8,128)(2,1)}, bf16[512,1024]{1,0:T(8,128)(2,1)}, u32[]{:S(2)}, u32[]{:S(2)}) collective-permute-start(bf16[512,1024]{1,0:T(8,128)(2,1)} %bitcast.60), channel_id=1, source_target_pairs={{0,3},{1,0},{2,1},{3,2},{4,7},{5,4},{6,5},{7,6},{8,11},{9,8},{10,9... | collective-permute-start | bytes 3145736 | tf_op jit(solution)/shard_map/ppermute | solution.py:684
  57.7 0.9 collective-permute-start.9
  58.6 3.7 %fusion = (f32[2,1024,128]{2,1,0:T(8,128)S(1)}, f32[2,1024,128]{2,1,0:T(8,128)S(1)}) fusion(f32[128]{0:T(128)S(1)} %compare_select_fusion.3, f32[128]{0:T(128)S(1)} %compare_select_fusion.4, f32[2,1024]{1,0:T(2,128)S(1)} %fusion.2), kind=kLoop, calls=%fused_computation.3 | loop fusion | flops 524288 | bytes 2106368 | tf_op jit(solution)/shard_map/mul | solution.py:679
  62.4 1.4 fusion.10
  63.7 10.7 %collective-permute-done.rest_1_ = bf16[512,1024]{1,0:T(8,128)(2,1)S(1)} collective-permute-done((bf16[512,1024]{1,0:T(8,128)(2,1)}, bf16[512,1024]{1,0:T(8,128)(2,1)S(1)}, u32[]{:S(2)}, u32[]{:S(2)}) %collective-permute-start) | collective-permute-done | bytes 1048608 | tf_op jit(solution)/shard_map/ppermute | solution.py:684
  74.5 1.0 copy-done.21
  75.4 1.0 copy-done.23
  76.5 1.0 copy-done.12
  77.5 1.0 copy-done.13
  78.6 1.2 copy-done.19
  79.8 1.2 copy-done.22
  81.0 1.2 copy-done.24
  82.3 13.9 %front.2 = (bf16[1,1024,1024]{2,1,0:T(8,128)(2,1)S(1)}, bf16[1,1024,1024]{2,1,0:T(8,128)(2,1)S(1)}, bf16[1,1024,1024]{2,1,0:T(8,128)(2,1)S(1)}, bf16[1,1024,1024...) custom-call(s32[1]{0:T(128)} %bitcast.z_ref, ...), custom_call_target="tpu_custom_call" | custom-call | flops 1024 | bytes 1024 | tf_op jit(solution)/shard_map/front/pallas_call | solution.py:200
  96.2 13.3 %attend.2 = (bf16[1,1024,256]{2,1,0:T(8,128)(2,1)S(1)}, bf16[1,3,1024,256]{3,2,1,0:T(8,128)(2,1)S(1)}, f32[3,8,256]{2,1,0:T(8,128)S(1)}) custom-call(s32[1]{0:T(128)} %bitcast.z_ref, bf16[1,1024,256]{2,1,0:T(8,128)(2,1)S(1)} %get-tuple-element.83.q_ref, bf16[1,1024,256]{2,1,0:T(8,128)(2,1)S(1)} %get-tuple-element.84.k_ref, ...), custom_call_target="tpu_custom_call" | custom-call | flops 1024 | bytes 1024 | tf_op jit(solution)/shard_map/attend/pallas_call | solution.py:312
  109.5 5.7 %grads_mlp0.1.rest_0_.sum_ref = bf16[1024,2048]{1,0:T(8,128)(2,1)S(1)} custom-call(bf16[1,1024,1024]{2,1,0:T(8,128)(2,1)S(1)} %get-tuple-element.92.n_ref.n0_ref, bf16[1,1024,1024]{2,1,0:T(8,128)(2,1)S(1)} %get-tuple-element.88.dup_ref, bf16[1,1024,1024]{2,1,0:T(8,128)(2,1)S(1)} %get-tuple-element.82.act_ref, ...), custom_call_target="tpu_custom_call" | custom-call | flops 1024 | bytes 1024 | tf_op jit(solution)/shard_map/grads_mlp0/pallas_call | solution.py:417
  115.3 2.4 collective-permute-done.9.rest_3_
  117.8 22.2 %back.2 = (bf16[2048,1024]{1,0:T(8,128)(2,1)S(1)}, f32[8,1024]{1,0:T(8,128)S(1)}, f32[8,1024]{1,0:T(8,128)S(1)}) custom-call(s32[1]{0:T(128)} %bitcast.z_ref, bf16[1,1024,1024]{2,1,0:T(8,128)(2,1)S(1)} %get-tuple-element.82.act_ref, bf16[1,1024,256]{2,1,0:T(8,128)(2,1)S(1)} %get-tuple-element.87.rest_0_.mix_ref.mix0_ref, ...), custom_call_target="tpu_custom_call" | custom-call | flops 1024 | bytes 1024 | tf_op jit(solution)/shard_map/back/pallas_call | solution.py:368
  140.0 2.1 copy-done.1
  142.1 0.9 copy-done.9
  143.7 15.1 %front.3 = (bf16[1,1024,1024]{2,1,0:T(8,128)(2,1)}, bf16[1,1024,1024]{2,1,0:T(8,128)(2,1)}, bf16[1,1024,1024]{2,1,0:T(8,128)(2,1)}, bf16[1,1024,1024]{2,1,0:T(8,...) custom-call(s32[1]{0:T(128)} %bitcast.z_ref, ...), custom_call_target="tpu_custom_call" | custom-call | flops 1024 | bytes 1024 | tf_op jit(solution)/shard_map/front/pallas_call | solution.py:200
  158.8 1.8 copy-done.5
  160.6 8.4 %grads_mlp1.1 = (bf16[512,2048]{1,0:T(8,128)(2,1)S(1)}, bf16[512,2048]{1,0:T(8,128)(2,1)S(1)}) custom-call(s32[1]{0:T(128)} %bitcast.8.c_ref, bf16[1,1024,1024]{2,1,0:T(8,128)(2,1)S(1)} %copy-done.5, bf16[1,1024,1024]{2,1,0:T(8,128)(2,1)} %get-tuple-element.101.dup_ref, bf16[1,1024,1024]{2,1,0:T(8,128)(2,1)} %get-tuple-element.95.act_ref, ...), custom_call_target="tpu_custom_call" | custom-call | flops 1024 | bytes 1024 | tf_op jit(solution)/shard_map/grads_mlp1/pallas_call | solution.py:433
  169.2 13.3 %attend.3 = (bf16[1,1024,256]{2,1,0:T(8,128)(2,1)S(1)}, bf16[1,3,1024,256]{3,2,1,0:T(8,128)(2,1)S(1)}, f32[3,8,256]{2,1,0:T(8,128)S(1)}) custom-call(s32[1]{0:T(128)} %bitcast.z_ref, bf16[1,1024,256]{2,1,0:T(8,128)(2,1)S(1)} %get-tuple-element.96.q_ref, bf16[1,1024,256]{2,1,0:T(8,128)(2,1)S(1)} %get-tuple-element.97.k_ref, ...), custom_call_target="tpu_custom_call" | custom-call | flops 1024 | bytes 1024 | tf_op jit(solution)/shard_map/attend/pallas_call | solution.py:312
  182.5 1.1 copy-done.7
  183.6 2.1 add_after.1.rest_0_
  185.8 10.6 %grads_att.1 = (bf16[512,1024]{1,0:T(8,128)(2,1)}, bf16[512,1024]{1,0:T(8,128)(2,1)}) custom-call(s32[1]{0:T(128)} %bitcast.8.c_ref, bf16[1,1024,1024]{2,1,0:T(8,128)(2,1)} %copy-done.4, bf16[1,1024,1024]{2,1,0:T(8,128)(2,1)} %get-tuple-element.100.n_ref.n1_ref, bf16[1,3,1024,256]{3,2,1,0:T(8,128)(2,1)} %copy-done.6, bf16[1,3,1024,256]{3,2,1,0:T(8,128)(2,1)} %copy-done.7, ...), custom_call_target="tpu_custom_call" | custom-call | flops 1024 | bytes 1024 | tf_op jit(solution)/shard_map/grads_att/pallas_call | solution.py:474
  196.5 12.9 %back.3 = (bf16[2048,1024]{1,0:T(8,128)(2,1)}, f32[8,1024]{1,0:T(8,128)}, f32[8,1024]{1,0:T(8,128)}) custom-call(s32[1]{0:T(128)} %bitcast.z_ref, bf16[1,1024,1024]{2,1,0:T(8,128)(2,1)} %get-tuple-element.95.act_ref, bf16[1,1024,256]{2,1,0:T(8,128)(2,1)} %copy-done.11, bf16[1,1024,1024]{2,1,0:T(8,128)(2,1)} %get-tuple-element.101.dup_ref, ...), custom_call_target="tpu_custom_call" | custom-call | flops 1024 | bytes 1024 | tf_op jit(solution)/shard_map/back/pallas_call | solution.py:368
  209.7 1.0 copy-done.27
  212.2 0.7 stack.28
  213.1 1.1 collective-permute-done.11.got_ref
  214.2 0.8 collective-permute-done.12.vb_ref
  214.9 1.3 to_xy.1
  216.2 7.8 %all-to-all-start = ((bf16[16,32,1152]{2,1,0:T(8,128)(2,1)}), bf16[16,32,1152]{2,1,0:T(8,128)(2,1)S(1)}, u32[]{:S(2)}, u32[]{:S(2)}) async-start(bf16[16,32,1152]{2,1,0:T(8,128)(2,1)} %to_xy.1), calls=%async_computation.2 | async-start | bytes 2359296 | tf_op jit(solution)/shard_map/all_to_all | solution.py:815
  224.1 1.9 to_y.1
  225.9 1.9 collective-permute-start.13
  227.8 2.7 collective-permute-start.14
  230.5 1.5 collective-permute-start.15
  232.0 11.0 %collective-permute-done.13.b_ref = bf16[32,2048]{1,0:T(8,128)(2,1)S(1)} collective-permute-done((bf16[32,2048]{1,0:T(8,128)(2,1)}, bf16[32,2048]{1,0:T(8,128)(2,1)S(1)}, u32[]{:S(2)}, u32[]{:S(2)}) %collective-permute-start.13) | collective-permute-done | bytes 131104 | tf_op jit(solution)/shard_map/ppermute | solution.py:684
  243.0 3.4 %collective-permute-done.14.c_ref = bf16[32,2048]{1,0:T(8,128)(2,1)S(1)} collective-permute-done((bf16[32,2048]{1,0:T(8,128)(2,1)}, bf16[32,2048]{1,0:T(8,128)(2,1)S(1)}, u32[]{:S(2)}, u32[]{:S(2)}) %collective-permute-start.14) | collective-permute-done | bytes 131104 | tf_op jit(solution)/shard_map/ppermute | solution.py:684
  246.4 0.6 copy-done.31
  247.4 2.3 to_z.1
  249.8 1.6 collective-permute-start.16
  251.3 7.6 %all-to-all-start.1 = ((bf16[4,8,1920]{2,1,0:T(8,128)(2,1)}), bf16[4,8,1920]{2,1,0:T(8,128)(2,1)S(1)}, u32[]{:S(2)}, u32[]{:S(2)}) async-start(bf16[4,8,1920]{2,1,0:T(8,128)(2,1)} %get-tuple-element.126), calls=%async_computation.4 | async-start | bytes 245760 | tf_op jit(solution)/shard_map/all_to_all | solution.py:822
  258.9 2.8 finish.2
  261.7 4.9 %all-to-all-done.1.home_ref = bf16[4,8,1920]{2,1,0:T(8,128)(2,1)S(1)} async-done(((bf16[4,8,1920]{2,1,0:T(8,128)(2,1)}), bf16[4,8,1920]{2,1,0:T(8,128)(2,1)S(1)}, u32[]{:S(2)}, u32[]{:S(2)}) %all-to-all-start.1) | async-done | bytes 122912 | tf_op jit(solution)/shard_map/all_to_all | solution.py:822
  266.7 0.6 copy-done.29
  267.3 1.6 home.1
  268.9 0.7 slice.88
  269.6 0.6 slice.87
  270.2 6.4 %reduce-scatter.6.cloned.1.call-done = bf16[512,1024]{1,0:T(8,128)(2,1)} async-done(((bf16[2048,1024]{1,0:T(8,128)(2,1)}), bf16[512,1024]{1,0:T(8,128)(2,1)}) %reduce-scatter.6.cloned.1.call-update) | async-done | bytes 1048592 | tf_op jit(solution)/shard_map/reduce_scatter | solution.py:778
  276.6 2.8 finish.3
  (138 shorter events, 5.8 us)
Async XLA Ops:
  7.2 69.3 %all-gather.2.cloned.1.call-start = ((), (), s32[]{:S(2)}) async-start(), calls=%async_computation.5 | async-start | bytes 6758400 | tf_op jit(solution)/shard_map/all_gather | solution.py:737
  8.9 11.8 %collective-permute-start.6 = (bf16[40,1024]{1,0:T(8,128)(2,1)}, bf16[40,1024]{1,0:T(8,128)(2,1)S(1)}, u32[]{:S(2)}, u32[]{:S(2)}) collective-permute-start(bf16[40,1024]{1,0:T(8,128)(2,1)} %get-tuple-element.79), channel_id=1, source_target_pairs={{0,0},{1,4},{2,8},{3,12},{4,16},{5,20},{6,24},{7,28},{8,32},{9,36}... | collective-permute-start | bytes 245768 | tf_op jit(solution)/shard_map/ppermute | solution.py:727
  10.4 9.7 %collective-permute-start.3 = (bf16[8,1920]{1,0:T(8,128)(2,1)}, bf16[8,1920]{1,0:T(8,128)(2,1)S(1)}, u32[]{:S(2)}, u32[]{:S(2)}) collective-permute-start(bf16[8,1920]{1,0:T(8,128)(2,1)} %get-tuple-element.76), channel_id=1, source_target_pairs={{0,1},{1,2},{2,3},{3,0},{4,5},{5,6},{6,7},{7,4},{8,9},{9,10},{10,1... | collective-permute-start | bytes 92168 | tf_op jit(solution)/shard_map/ppermute | solution.py:684
  12.9 7.3 %collective-permute-start.4 = (bf16[8,1920]{1,0:T(8,128)(2,1)}, bf16[8,1920]{1,0:T(8,128)(2,1)S(1)}, u32[]{:S(2)}, u32[]{:S(2)}) collective-permute-start(bf16[8,1920]{1,0:T(8,128)(2,1)} %get-tuple-element.77), channel_id=1, source_target_pairs={{0,2},{1,3},{2,0},{3,1},{4,6},{5,7},{6,4},{7,5},{8,10},{9,11},{10,... | collective-permute-start | bytes 92168 | tf_op jit(solution)/shard_map/ppermute | solution.py:684
  16.4 11.5 %copy-start.34 = (s32[2,1,1024]{2,1,0:T(1,128)S(1)}, s32[2,1,1024]{2,1,0:T(1,128)}, u32[]{:S(2)}) copy-start(s32[2,1,1024]{2,1,0:T(1,128)} %param.15) | copy-start | bytes 24580
  16.5 4.3 %collective-permute-start.5 = (bf16[8,1920]{1,0:T(8,128)(2,1)}, bf16[8,1920]{1,0:T(8,128)(2,1)S(1)}, u32[]{:S(2)}, u32[]{:S(2)}) collective-permute-start(bf16[8,1920]{1,0:T(8,128)(2,1)} %get-tuple-element.78), channel_id=1, source_target_pairs={{0,3},{1,0},{2,1},{3,2},{4,7},{5,4},{6,5},{7,6},{8,11},{9,8},{10,9... | collective-permute-start | bytes 92168 | tf_op jit(solution)/shard_map/ppermute | solution.py:684
  20.2 0.6 copy-start.38
  20.7 0.6 copy-start.33
  23.1 173.4 %reduce-scatter.4.cloned.1.call-start = ((), (), s32[]{:S(2)}) async-start(), calls=%async_computation.6 | async-start | bytes 5242880 | tf_op jit(solution)/shard_map/reduce_scatter | solution.py:765
  23.1 27.8 %collective-permute-start.1 = (bf16[512,1024]{1,0:T(8,128)(2,1)}, bf16[512,1024]{1,0:T(8,128)(2,1)S(1)}, u32[]{:S(2)}, u32[]{:S(2)}) collective-permute-start(bf16[512,1024]{1,0:T(8,128)(2,1)} %bitcast.56), channel_id=1, source_target_pairs={{0,2},{1,3},{2,0},{3,1},{4,6},{5,7},{6,4},{7,5},{8,10},{9,11},{10,... | collective-permute-start | bytes 3145736 | tf_op jit(solution)/shard_map/ppermute | solution.py:684
  25.9 48.6 %collective-permute-start = (bf16[512,1024]{1,0:T(8,128)(2,1)}, bf16[512,1024]{1,0:T(8,128)(2,1)S(1)}, u32[]{:S(2)}, u32[]{:S(2)}) collective-permute-start(bf16[512,1024]{1,0:T(8,128)(2,1)} %bitcast.57), channel_id=1, source_target_pairs={{0,3},{1,0},{2,1},{3,2},{4,7},{5,4},{6,5},{7,6},{8,11},{9,8},{10,9... | collective-permute-start | bytes 3145736 | tf_op jit(solution)/shard_map/ppermute | solution.py:684
  27.0 48.5 %collective-permute-start.2 = (bf16[512,1024]{1,0:T(8,128)(2,1)}, bf16[512,1024]{1,0:T(8,128)(2,1)S(1)}, u32[]{:S(2)}, u32[]{:S(2)}) collective-permute-start(bf16[512,1024]{1,0:T(8,128)(2,1)} %bitcast.58), channel_id=1, source_target_pairs={{0,1},{1,2},{2,3},{3,0},{4,5},{5,6},{6,7},{7,4},{8,9},{9,10},{10,1... | collective-permute-start | bytes 3145736 | tf_op jit(solution)/shard_map/ppermute | solution.py:684
  29.1 29.5 %copy-start.40 = (s32[2,1,1024]{2,1,0:T(1,128)S(1)}, s32[2,1,1024]{2,1,0:T(1,128)}, u32[]{:S(2)}) copy-start(s32[2,1,1024]{2,1,0:T(1,128)} %param.16) | copy-start | bytes 24580
  51.0 1.0 copy-start.18
  54.0 61.3 %collective-permute-start.7 = (bf16[512,1024]{1,0:T(8,128)(2,1)}, bf16[512,1024]{1,0:T(8,128)(2,1)}, u32[]{:S(2)}, u32[]{:S(2)}) collective-permute-start(bf16[512,1024]{1,0:T(8,128)(2,1)} %bitcast.60), channel_id=1, source_target_pairs={{0,3},{1,0},{2,1},{3,2},{4,7},{5,4},{6,5},{7,6},{8,11},{9,8},{10,9... | collective-permute-start | bytes 3145736 | tf_op jit(solution)/shard_map/ppermute | solution.py:684
  57.7 57.6 %collective-permute-start.8 = (bf16[512,1024]{1,0:T(8,128)(2,1)}, bf16[512,1024]{1,0:T(8,128)(2,1)}, u32[]{:S(2)}, u32[]{:S(2)}) collective-permute-start(bf16[512,1024]{1,0:T(8,128)(2,1)} %bitcast.61), channel_id=1, source_target_pairs={{0,2},{1,3},{2,0},{3,1},{4,6},{5,7},{6,4},{7,5},{8,10},{9,11},{10,... | collective-permute-start | bytes 3145736 | tf_op jit(solution)/shard_map/ppermute | solution.py:684
  57.7 60.0 %collective-permute-start.9 = (bf16[512,1024]{1,0:T(8,128)(2,1)}, bf16[512,1024]{1,0:T(8,128)(2,1)}, u32[]{:S(2)}, u32[]{:S(2)}) collective-permute-start(bf16[512,1024]{1,0:T(8,128)(2,1)} %bitcast.62), channel_id=1, source_target_pairs={{0,1},{1,2},{2,3},{3,0},{4,5},{5,6},{6,7},{7,4},{8,9},{9,10},{10,1... | collective-permute-start | bytes 3145736 | tf_op jit(solution)/shard_map/ppermute | solution.py:684
  62.3 14.1 %copy-start.2 = (bf16[2,256,1024]{2,1,0:T(8,128)(2,1)S(1)}, bf16[2,256,1024]{2,1,0:T(8,128)(2,1)}, u32[]{:S(2)}) copy-start(bf16[2,256,1024]{2,1,0:T(8,128)(2,1)} %pack.2) | copy-start | bytes 3145732
  74.5 1.0 copy-start.21
  75.4 1.0 copy-start.23
  76.5 1.0 copy-start.12
  77.5 1.0 copy-start.13
  78.6 1.2 copy-start.19
  79.8 1.2 copy-start.22
  81.0 1.2 copy-start.24
  82.3 13.9 %copy-start.14 = (f32[1,1024,128]{2,1,0:T(8,128)S(1)}, f32[1,1024,128]{2,1,0:T(8,128)}, u32[]{:S(2)}) copy-start(f32[1,1024,128]{2,1,0:T(8,128)} %get-tuple-element.174.rest_5_.cos_ref) | copy-start | bytes 1572868
  96.1 19.1 %copy-start.3 = (bf16[1,1024,1024]{2,1,0:T(8,128)(2,1)}, bf16[1,1024,1024]{2,1,0:T(8,128)(2,1)S(1)}, u32[]{:S(2)}) copy-start(bf16[1,1024,1024]{2,1,0:T(8,128)(2,1)S(1)} %get-tuple-element.93.cot_ref.cot0_ref) | copy-start | bytes 6291460
  96.1 19.1 %copy-start.4 = (bf16[1,1024,1024]{2,1,0:T(8,128)(2,1)}, bf16[1,1024,1024]{2,1,0:T(8,128)(2,1)S(1)}, u32[]{:S(2)}) copy-start(bf16[1,1024,1024]{2,1,0:T(8,128)(2,1)S(1)} %get-tuple-element.92.n_ref.n0_ref) | copy-start | bytes 6291460
  96.1 21.6 %copy-start.8 = (bf16[256,1024]{1,0:T(8,128)(2,1)}, bf16[256,1024]{1,0:T(8,128)(2,1)S(1)}, u32[]{:S(2)}) copy-start(bf16[256,1024]{1,0:T(8,128)(2,1)S(1)} %get-tuple-element.81.wo_ref.rest_5_) | copy-start | bytes 1572868
  96.1 46.0 %copy-start.26 = (f32[8,1024]{1,0:T(8,128)}, f32[8,1024]{1,0:T(8,128)S(1)}, u32[]{:S(2)}) copy-start(f32[8,1024]{1,0:T(8,128)S(1)} %get-tuple-element.80.rest_6_.vec_ref) | copy-start | bytes 98308
  109.5 8.3 %copy-start.6 = (bf16[1,3,1024,256]{3,2,1,0:T(8,128)(2,1)}, bf16[1,3,1024,256]{3,2,1,0:T(8,128)(2,1)S(1)}, u32[]{:S(2)}) copy-start(bf16[1,3,1024,256]{3,2,1,0:T(8,128)(2,1)S(1)} %get-tuple-element.89.dqkv_ref.dqkv0_ref) | copy-start | bytes 4718596
  109.5 8.2 %copy-start.10 = (bf16[1,1024,256]{2,1,0:T(8,128)(2,1)}, bf16[1,1024,256]{2,1,0:T(8,128)(2,1)S(1)}, u32[]{:S(2)}) copy-start(bf16[1,1024,256]{2,1,0:T(8,128)(2,1)S(1)} %get-tuple-element.87.rest_0_.mix_ref.mix0_ref) | copy-start | bytes 1572868
  109.5 8.2 %slice-start = ((s8[6553600]{0:T(1024)(128)(4,1)}), s8[4194304]{0:T(1024)(128)(4,1)S(1)}, s32[]{:S(2)}) async-start(s8[6553600]{0:T(1024)(128)(4,1)} %bitcast.53), calls=%async_computation.9 | async-start | bytes 8388608
  109.5 8.2 %slice-start.1 = ((s8[6553600]{0:T(1024)(128)(4,1)}), s8[2359296]{0:T(1024)(128)(4,1)S(1)}, s32[]{:S(2)}) async-start(s8[6553600]{0:T(1024)(128)(4,1)} %bitcast.53), calls=%async_computation.10 | async-start | bytes 4718592
  115.3 24.7 %copy-start = (bf16[1024,2048]{1,0:T(8,128)(2,1)}, bf16[1024,2048]{1,0:T(8,128)(2,1)S(1)}, u32[]{:S(2)}) copy-start(bf16[1024,2048]{1,0:T(8,128)(2,1)S(1)} %grads_mlp0.1.rest_0_.sum_ref) | copy-start | bytes 12582916
  140.0 2.1 copy-start.1
  142.0 1.0 copy-start.9
  142.0 1.2 copy-start.15
  142.0 1.4 copy-start.16
  142.0 1.7 copy-start.17
  142.1 82.0 %reduce-scatter.8.cloned.1.call-start = ((), (), s32[]{:S(2)}) async-start(), calls=%async_computation.8 | async-start | bytes 2621440 | tf_op jit(solution)/shard_map/reduce_scatter | solution.py:774
  158.8 10.2 %copy-start.25 = (f32[1,1024,128]{2,1,0:T(8,128)}, f32[1,1024,128]{2,1,0:T(8,128)S(1)}, u32[]{:S(2)}) copy-start(f32[1,1024,128]{2,1,0:T(8,128)S(1)} %get-tuple-element.107.stat_ref) | copy-start | bytes 1572868
  158.8 1.8 copy-start.5
  169.1 14.6 %collective-permute-start.10 = (bf16[512,2048]{1,0:T(8,128)(2,1)S(1)}, bf16[512,2048]{1,0:T(8,128)(2,1)S(1)}, u32[]{:S(2)}, u32[]{:S(2)}) collective-permute-start(bf16[512,2048]{1,0:T(8,128)(2,1)S(1)} %get-tuple-element.108), channel_id=1, source_target_pairs={{0,4},{4,0},{1,5},{5,1},{2,6},{6,2},{3,7},{7,3},{8,12},{12,8},{9,1... | collective-permute-start | bytes 6291464 | tf_op jit(solution)/shard_map/ppermute | solution.py:684
  182.5 1.1 copy-start.7
  183.6 2.1 copy-start.11
  185.8 90.8 %reduce-scatter.6.cloned.1.call-start = ((), (), s32[]{:S(2)}) async-start(), calls=%async_computation.7 | async-start | bytes 5242880 | tf_op jit(solution)/shard_map/reduce_scatter | solution.py:778
  209.4 1.2 copy-start.27
  209.4 2.5 copy-start.36
  209.5 2.6 copy-start.35
  209.5 5.5 %copy-start.20 = (bf16[512,1024]{1,0:T(8,128)(2,1)S(1)}, bf16[512,1024]{1,0:T(8,128)(2,1)}, u32[]{:S(2)}) copy-start(bf16[512,1024]{1,0:T(8,128)(2,1)} %get-tuple-element.109.rest_1_.own_ref) | copy-start | bytes 3145732
  211.1 3.0 %collective-permute-start.11 = (bf16[512,1024]{1,0:T(8,128)(2,1)}, bf16[512,1024]{1,0:T(8,128)(2,1)S(1)}, u32[]{:S(2)}, u32[]{:S(2)}) collective-permute-start(bf16[512,1024]{1,0:T(8,128)(2,1)} %get-tuple-element.113), channel_id=1, source_target_pairs={{0,4},{4,0},{1,5},{5,1},{2,6},{6,2},{3,7},{7,3},{8,12},{12,8},{9,1... | collective-permute-start | bytes 3145736 | tf_op jit(solution)/shard_map/ppermute | solution.py:684
  213.0 2.0 collective-permute-start.12
  216.2 30.1 %all-to-all-start = ((bf16[16,32,1152]{2,1,0:T(8,128)(2,1)}), bf16[16,32,1152]{2,1,0:T(8,128)(2,1)S(1)}, u32[]{:S(2)}, u32[]{:S(2)}) async-start(bf16[16,32,1152]{2,1,0:T(8,128)(2,1)} %to_xy.1), calls=%async_computation.2 | async-start | bytes 2359296 | tf_op jit(solution)/shard_map/all_to_all | solution.py:815
  225.9 17.1 %collective-permute-start.13 = (bf16[32,2048]{1,0:T(8,128)(2,1)}, bf16[32,2048]{1,0:T(8,128)(2,1)S(1)}, u32[]{:S(2)}, u32[]{:S(2)}) collective-permute-start(bf16[32,2048]{1,0:T(8,128)(2,1)} %get-tuple-element.123), channel_id=1, source_target_pairs={{0,8},{8,16},{16,24},{24,0},{1,9},{9,17},{17,25},{25,1},{2,10},{10... | collective-permute-start | bytes 393224 | tf_op jit(solution)/shard_map/ppermute | solution.py:684
  227.8 18.5 %collective-permute-start.14 = (bf16[32,2048]{1,0:T(8,128)(2,1)}, bf16[32,2048]{1,0:T(8,128)(2,1)S(1)}, u32[]{:S(2)}, u32[]{:S(2)}) collective-permute-start(bf16[32,2048]{1,0:T(8,128)(2,1)} %get-tuple-element.124), channel_id=1, source_target_pairs={{0,16},{8,24},{16,0},{24,8},{1,17},{9,25},{17,1},{25,9},{2,18},{10... | collective-permute-start | bytes 393224 | tf_op jit(solution)/shard_map/ppermute | solution.py:684
  230.5 15.9 %collective-permute-start.15 = (bf16[32,2048]{1,0:T(8,128)(2,1)}, bf16[32,2048]{1,0:T(8,128)(2,1)S(1)}, u32[]{:S(2)}, u32[]{:S(2)}) collective-permute-start(bf16[32,2048]{1,0:T(8,128)(2,1)} %get-tuple-element.125), channel_id=1, source_target_pairs={{0,24},{8,0},{16,8},{24,16},{1,25},{9,1},{17,9},{25,17},{2,26},{10... | collective-permute-start | bytes 393224 | tf_op jit(solution)/shard_map/ppermute | solution.py:684
  243.0 3.4 %copy-start.30 = (bf16[32,2048]{1,0:T(8,128)(2,1)}, bf16[32,2048]{1,0:T(8,128)(2,1)S(1)}, u32[]{:S(2)}) copy-start(bf16[32,2048]{1,0:T(8,128)(2,1)S(1)} %collective-permute-done.13.b_ref) | copy-start | bytes 393220
  246.3 0.7 copy-start.31
  246.4 0.7 copy-start.32
  246.4 1.1 copy-start.28
  249.8 19.2 %collective-permute-start.16 = (f32[40,1024]{1,0:T(8,128)}, f32[40,1024]{1,0:T(8,128)S(1)}, u32[]{:S(2)}, u32[]{:S(2)}) collective-permute-start(f32[40,1024]{1,0:T(8,128)} %get-tuple-element.131), channel_id=1, source_target_pairs={{0,0},{4,1},{8,2},{12,3},{16,4},{20,5},{24,6},{28,7},{32,8},{36,9}... | collective-permute-start | bytes 491528 | tf_op jit(solution)/shard_map/ppermute | solution.py:823
  251.3 15.3 %all-to-all-start.1 = ((bf16[4,8,1920]{2,1,0:T(8,128)(2,1)}), bf16[4,8,1920]{2,1,0:T(8,128)(2,1)S(1)}, u32[]{:S(2)}, u32[]{:S(2)}) async-start(bf16[4,8,1920]{2,1,0:T(8,128)(2,1)} %get-tuple-element.126), calls=%async_computation.4 | async-start | bytes 245760 | tf_op jit(solution)/shard_map/all_to_all | solution.py:822
  266.7 0.6 copy-start.29
  (2 other events, 1.2 us)
Sparse Core Ops, SparseCore 0:
  23.2 51.6 all-gather.1
  142.2 48.7 reduce-scatter.3
  193.5 29.1 reduce-scatter.7
  225.0 51.5 reduce-scatter.5
